TPU v7x, 32 devices: a whole 2x2x4 slice. The times are simulated.
32 devices in a mesh: sta: 8 (over y, x, core), tm: 4 (over z).
Axes of the slice: x: 2, y: 2, z: 4, core: 2. Of those that a mesh axis runs over, the one named last changes fastest.
Arguments:
- strain: bfloat16 [256, 4096], P('sta', 'tm'), may hold values from -1800 to 1800
- plan: int32 [4], replicated, may hold values from 1 to 7, as said below
Outputs:
- correlations: float32 [4096, 1024], P('tm', 'sta')
Inputs may be any that keep to these rules, and one draw needn't show every extreme that they name: In round r block b is paired with block b XOR plan[r]; the 4 keys are distinct, and every draw holds the keys 1 and 7.
All inputs are finite; a program needn't handle non-finite values.
Results may differ from a plain program's by a relative error of at most 0.0041.
Values may be sent and summed in bfloat16 or wider, within the bound.
No kernel may reach another device: no remote copies, remote signals or barrier semaphores. Data moves between devices by JAX's collectives and lax.ppermute only.
A program may use at most 192 MiB of HBM per device.

v0:
```python
import math

import jax
import jax.numpy as jnp
from jax import lax
from jax.sharding import PartitionSpec as P

SOURCES = 4
MAX_LAG = 512
ROUNDS = 4
LAGS = 1024


epsilon = 1e-06


def partner(block, axis, stride):
    count = lax.axis_size(axis)
    route = []
    for low in range(count):
        high = low | 1 << stride
        if high != low and high < count:
            route += [(low, high), (high, low)]
    return lax.ppermute(block, axis, route)


def extended(block, sides, width):
    for axis, dim in sides:
        count = lax.axis_size(axis)
        forward = [(i, i + 1) for i in range(count - 1)]
        backward = [(target, source) for source, target in forward]
        low = lax.ppermute(
            lax.slice_in_dim(block, block.shape[dim] - width, None, axis=dim), axis, forward
        )
        high = lax.ppermute(lax.slice_in_dim(block, 0, width, axis=dim), axis, backward)
        block = jnp.concatenate([low, block, high], axis=dim)
    return block


def build_table(lines, width):
    line_len = lines.shape[-1]
    segments = line_len // width
    lead = lines.shape[:-1]
    earlier = jnp.pad(lines, [(0, 0)] * len(lead) + [(width, 0)])[..., :line_len]
    paired = jnp.concatenate(
        [earlier.reshape(lead + (segments, width)), lines.reshape(lead + (segments, width))],
        axis=-1,
    )
    diagonal_line = paired[..., 1:]
    repeated = jnp.tile(diagonal_line, (1,) * (len(lead) + 1) + (width,))
    flattened = lax.slice_in_dim(
        repeated, width - 1, width - 1 + width * (2 * width - 2), axis=len(lead) + 1
    )
    skewed = flattened.reshape(lead + (segments, width, 2 * width - 2))[..., :width]
    return jnp.swapaxes(skewed, -3, -2)


def correlate(row_count, table, first_source, whitened, width, norm_factor):
    channel_count, series_len = whitened.shape
    segments = series_len // width
    round_count = table.shape[0]
    folded = whitened.reshape(channel_count, segments, width)

    def one_block(block_index):
        first_row = block_index * width
        source_index = first_row // LAGS - first_source
        low_lag = first_row % LAGS
        seg_start = (LAGS - low_lag) // width
        zero = jnp.zeros((), jnp.int32)
        piece = lax.dynamic_slice(
            table,
            (zero, source_index, zero, seg_start, zero),
            (round_count, 1, width, segments, width),
        )
        piece = piece[:, 0]
        product = lax.dot_general(
            piece, folded, (((2, 3), (1, 2)), ((), ())), preferred_element_type=jnp.float32
        )
        return norm_factor * jnp.transpose(product, (1, 2, 0)).reshape(
            width, channel_count * round_count
        )

    blocks_out = lax.map(one_block, jnp.arange(row_count // width, dtype=jnp.int32))
    return blocks_out.reshape(row_count, -1)


def local(strain, plan):
    channel_count, tile_len = strain.shape
    widened = strain.astype(jnp.float32)
    energy = lax.psum(jnp.sum(widened * widened, axis=1), "tm")
    sample_count = tile_len * lax.axis_size("tm")
    whitened = (widened * lax.rsqrt(energy / sample_count + epsilon)[:, None]).astype(jnp.bfloat16)
    sources = whitened.reshape(SOURCES, channel_count // SOURCES, tile_len)[:, 0, :]
    hop_count = lax.axis_size("sta").bit_length() - 1
    per_round = []
    for round_index in range(ROUNDS):
        current = sources
        for bit_number in range(hop_count):
            arrived = partner(current, "sta", bit_number)
            flagged = jnp.bitwise_and(jnp.right_shift(plan[round_index], bit_number), 1) == 1
            current = jnp.where(flagged, arrived, current)
        per_round.append(current)
    paired_block = jnp.stack(per_round)
    block_rows = SOURCES * LAGS // lax.axis_size("tm")
    width = math.gcd(math.gcd(block_rows, LAGS), math.gcd(tile_len, 128))
    norm_factor = 1.0 / math.sqrt(sample_count)
    padded = extended(paired_block, (("tm", 2),), MAX_LAG)
    table = build_table(padded, width)
    return lax.psum_scatter(
        correlate(block_rows * lax.axis_size("tm"), table, 0, whitened, width, norm_factor),
        "tm",
        scatter_dimension=0,
        tiled=True,
    )


def solution(mesh):
    in_specs = (P("sta", "tm"), P())
    out_specs = P("tm", "sta")
    return jax.shard_map(local, mesh=mesh, in_specs=in_specs, out_specs=out_specs, check_vma=False)
```

profile of v0, /device:TPU:0, one launch (start us, length us, event | category | flops | bytes accessed | tf_op | source)
XLA Modules:
  0.0 337.1 jit_solution(5546315364005178092)
XLA Ops:
  7.5 13.5 %psum.7 = f32[32]{0:T(128)S(1)} all-reduce(f32[32]{0:T(128)S(1)} %fusion.6), channel_id=1, replica_groups=mesh['sta'=8,'tm'=4] {'tm'}, use_global_device_ids=true, to_apply=%region_1.0 | all-reduce | flops 32 | bytes 256 | tf_op jit(solution)/shard_map/psum | solution.py:90
  44.2 4.5 %collective-permute-start.9 = (bf16[4,4,512]{2,1,0:T(4,128)(2,1)S(1)}, bf16[4,4,512]{2,1,0:T(4,128)(2,1)S(1)}, u32[]{:S(2)}, u32[]{:S(2)}) collective-permute-start(bf16[4,4,512]{2,1,0:T(4,128)(2,1)S(1)} %get-tuple-element.116), channel_id=1, source_target_pairs={{0,1},{1,2},{2,3},{4,5},{5,6},{6,7},{8,9},{9,10},{10,11},{12,13},{... | collective-permute-start | bytes 49160 | tf_op jit(solution)/shard_map/ppermute | solution.py:32
  50.5 5.9 %tile.4 = bf16[4,4,16,128,255]{4,3,2,1,0:T(8,128)(2,1)} broadcast(bf16[4,4,16,255]{3,2,1,0:T(8,128)(2,1)S(1)} %pad_maximum_fusion), dimensions={0,1,2,4} | broadcast | bytes 16842240 | tf_op jit(solution)/shard_map/tile | solution.py:50
  56.4 28.1 %tile.10 = bf16[4,4,16,32640]{3,2,1,0:T(8,128)(2,1)} reshape(bf16[4,4,16,128,255]{4,3,2,1,0:T(8,128)(2,1)} %tile.4) | data formatting | bytes 33423360 | tf_op jit(solution)/shard_map/tile | solution.py:50
  84.6 15.3 %slice.55 = bf16[4,4,16,32512]{3,2,1,0:T(8,128)(2,1)} slice(bf16[4,4,16,32640]{3,2,1,0:T(8,128)(2,1)} %tile.10), slice={[0:4], [0:4], [0:16], [127:32639]} | slice | bytes 33292288 | tf_op jit(solution)/shard_map/slice | solution.py:51
  99.9 58.2 %reshape.117 = bf16[4,4,16,128,254]{4,3,2,1,0:T(8,128)(2,1)} reshape(bf16[4,4,16,32512]{3,2,1,0:T(8,128)(2,1)} %slice.55) | data formatting | bytes 33292288 | tf_op jit(solution)/shard_map/reshape | solution.py:54
  158.1 10.5 %slice_bitcast_fusion = bf16[4,4,128,16,128]{4,2,3,1,0:T(8,128)(2,1)} fusion(bf16[4,4,16,128,254]{4,3,2,1,0:T(8,128)(2,1)} %reshape.117), kind=kLoop, calls=%fused_computation.8 | loop fusion | bytes 16777216 | tf_op jit(solution)/shard_map/transpose | solution.py:55
  168.6 118.7 %while.13 = (s32[]{:T(128)}, f32[32,128,128]{2,1,0:T(8,128)}, s32[32]{0:T(128)S(1)}, bf16[4,4,128,16,128]{4,2,3,1,0:T(8,128)(2,1)}, bf16[32,8,128]{2,0,1:T(8,128...) while((s32[]{:T(128)}, f32[32,128,128]{2,1,0:T(8,128)}, ...), condition=%wide.region_3.4_spmd, body=%wide.region_2.3_spmd.sunk | while | flops 33570860 | bytes 1573974 | solution.py:83
  169.8 1.6 fusion.17
  173.6 1.6 fusion.17
  177.3 1.6 fusion.17
  181.0 1.6 fusion.17
  192.1 1.6 fusion.17
  195.8 1.6 fusion.17
  206.9 1.6 fusion.17
  210.6 1.6 fusion.17
  214.3 1.6 fusion.17
  225.5 1.6 fusion.17
  229.2 1.6 fusion.17
  244.0 1.6 fusion.17
  247.7 1.6 fusion.17
  251.4 1.6 fusion.17
  273.7 1.6 fusion.17
  287.3 43.0 %reduce-scatter.2.cloned.1.call-done = f32[1024,128]{1,0:T(8,128)} async-done(((f32[4096,128]{1,0:T(8,128)}), f32[1024,128]{1,0:T(8,128)}) %reduce-scatter.2.cloned.1.call-update) | async-done | bytes 524304 | tf_op jit(solution)/shard_map/reduce_scatter | solution.py:109
  (193 shorter events, 90.1 us)
Async XLA Ops:
  6.5 323.7 %reduce-scatter.2.cloned.1.call-start = ((), (), s32[]{:S(2)}) async-start(), calls=%async_computation.1 | async-start | bytes 2621440 | tf_op jit(solution)/shard_map/reduce_scatter | solution.py:109
  21.9 4.1 %collective-permute-start = (bf16[4,1024]{1,0:T(4,128)(2,1)S(1)}, bf16[4,1024]{1,0:T(4,128)(2,1)S(1)}, u32[]{:S(2)}, u32[]{:S(2)}) collective-permute-start(bf16[4,1024]{1,0:T(4,128)(2,1)S(1)} %bitcast.73), channel_id=1, source_target_pairs={{0,4},{4,0},{8,12},{12,8},{16,20},{20,16},{24,28},{28,24},{1,5},{5... | collective-permute-start | bytes 24584 | tf_op jit(solution)/shard_map/ppermute | solution.py:24
  26.0 9.3 %collective-permute-start.7 = (bf16[4,1024]{1,0:T(4,128)(2,1)S(1)}, bf16[4,1024]{1,0:T(4,128)(2,1)S(1)}, u32[]{:S(2)}, u32[]{:S(2)}) collective-permute-start(bf16[4,1024]{1,0:T(4,128)(2,1)S(1)} %get-tuple-element.119), channel_id=1, source_target_pairs={{0,8},{8,0},{4,12},{12,4},{16,24},{24,16},{20,28},{28,20},{1,9},{9... | collective-permute-start | bytes 24584 | tf_op jit(solution)/shard_map/ppermute | solution.py:24
  32.7 4.2 %collective-permute-start.5 = (bf16[4,1024]{1,0:T(4,128)(2,1)S(1)}, bf16[4,1024]{1,0:T(4,128)(2,1)S(1)}, u32[]{:S(2)}, u32[]{:S(2)}) collective-permute-start(bf16[4,1024]{1,0:T(4,128)(2,1)S(1)} %get-tuple-element.120), channel_id=1, source_target_pairs={{0,8},{8,0},{4,12},{12,4},{16,24},{24,16},{20,28},{28,20},{1,9},{9... | collective-permute-start | bytes 24584 | tf_op jit(solution)/shard_map/ppermute | solution.py:24
  33.3 4.7 %collective-permute-start.3 = (bf16[4,1024]{1,0:T(4,128)(2,1)S(1)}, bf16[4,1024]{1,0:T(4,128)(2,1)S(1)}, u32[]{:S(2)}, u32[]{:S(2)}) collective-permute-start(bf16[4,1024]{1,0:T(4,128)(2,1)S(1)} %get-tuple-element.121), channel_id=1, source_target_pairs={{0,8},{8,0},{4,12},{12,4},{16,24},{24,16},{20,28},{28,20},{1,9},{9... | collective-permute-start | bytes 24584 | tf_op jit(solution)/shard_map/ppermute | solution.py:24
  34.8 4.3 %collective-permute-start.1 = (bf16[4,1024]{1,0:T(4,128)(2,1)S(1)}, bf16[4,1024]{1,0:T(4,128)(2,1)S(1)}, u32[]{:S(2)}, u32[]{:S(2)}) collective-permute-start(bf16[4,1024]{1,0:T(4,128)(2,1)S(1)} %get-tuple-element.118), channel_id=1, source_target_pairs={{0,8},{8,0},{4,12},{12,4},{16,24},{24,16},{20,28},{28,20},{1,9},{9... | collective-permute-start | bytes 24584 | tf_op jit(solution)/shard_map/ppermute | solution.py:24
  35.3 4.9 %collective-permute-start.8 = (bf16[4,1024]{1,0:T(4,128)(2,1)S(1)}, bf16[4,1024]{1,0:T(4,128)(2,1)S(1)}, u32[]{:S(2)}, u32[]{:S(2)}) collective-permute-start(bf16[4,1024]{1,0:T(4,128)(2,1)S(1)} %broadcast_select_fusion.1), channel_id=1, source_target_pairs={{0,16},{16,0},{4,20},{20,4},{8,24},{24,8},{12,28},{28,12},{1,17},{... | collective-permute-start | bytes 24584 | tf_op jit(solution)/shard_map/ppermute | solution.py:24
  36.9 3.7 %collective-permute-start.6 = (bf16[4,1024]{1,0:T(4,128)(2,1)S(1)}, bf16[4,1024]{1,0:T(4,128)(2,1)S(1)}, u32[]{:S(2)}, u32[]{:S(2)}) collective-permute-start(bf16[4,1024]{1,0:T(4,128)(2,1)S(1)} %broadcast_select_fusion.3), channel_id=1, source_target_pairs={{0,16},{16,0},{4,20},{20,4},{8,24},{24,8},{12,28},{28,12},{1,17},{... | collective-permute-start | bytes 24584 | tf_op jit(solution)/shard_map/ppermute | solution.py:24
  38.0 3.7 %collective-permute-start.4 = (bf16[4,1024]{1,0:T(4,128)(2,1)S(1)}, bf16[4,1024]{1,0:T(4,128)(2,1)S(1)}, u32[]{:S(2)}, u32[]{:S(2)}) collective-permute-start(bf16[4,1024]{1,0:T(4,128)(2,1)S(1)} %broadcast_select_fusion.5), channel_id=1, source_target_pairs={{0,16},{16,0},{4,20},{20,4},{8,24},{24,8},{12,28},{28,12},{1,17},{... | collective-permute-start | bytes 24584 | tf_op jit(solution)/shard_map/ppermute | solution.py:24
  39.1 3.7 %collective-permute-start.2 = (bf16[4,1024]{1,0:T(4,128)(2,1)S(1)}, bf16[4,1024]{1,0:T(4,128)(2,1)S(1)}, u32[]{:S(2)}, u32[]{:S(2)}) collective-permute-start(bf16[4,1024]{1,0:T(4,128)(2,1)S(1)} %broadcast_select_fusion.7), channel_id=1, source_target_pairs={{0,16},{16,0},{4,20},{20,4},{8,24},{24,8},{12,28},{28,12},{1,17},{... | collective-permute-start | bytes 24584 | tf_op jit(solution)/shard_map/ppermute | solution.py:24
  42.9 5.9 %collective-permute-start.10 = (bf16[4,4,512]{2,1,0:T(4,128)(2,1)S(1)}, bf16[4,4,512]{2,1,0:T(4,128)(2,1)S(1)}, u32[]{:S(2)}, u32[]{:S(2)}) collective-permute-start(bf16[4,4,512]{2,1,0:T(4,128)(2,1)S(1)} %get-tuple-element.117), channel_id=1, source_target_pairs={{1,0},{2,1},{3,2},{5,4},{6,5},{7,6},{9,8},{10,9},{11,10},{13,12},{... | collective-permute-start | bytes 49160 | tf_op jit(solution)/shard_map/ppermute | solution.py:35
  44.2 6.0 %collective-permute-start.9 = (bf16[4,4,512]{2,1,0:T(4,128)(2,1)S(1)}, bf16[4,4,512]{2,1,0:T(4,128)(2,1)S(1)}, u32[]{:S(2)}, u32[]{:S(2)}) collective-permute-start(bf16[4,4,512]{2,1,0:T(4,128)(2,1)S(1)} %get-tuple-element.116), channel_id=1, source_target_pairs={{0,1},{1,2},{2,3},{4,5},{5,6},{6,7},{8,9},{9,10},{10,11},{12,13},{... | collective-permute-start | bytes 49160 | tf_op jit(solution)/shard_map/ppermute | solution.py:32
Sparse Core Ops, SparseCore 0:
  287.4 42.8 reduce-scatter.1
where the time goes:
time: 342 us; the launch traced here: 337 us
  local copies, waits for them, and re-layouts  164 us (48%)
  matrix products  52.2 us (15%)
  waiting for transfers between devices  47 us (14%)
  loops' own time  22.4 us (7%)
  between operations  21.2 us (6%)
  starting transfers between devices  14.9 us (4%)
  blocking collectives  13.5 us (4%)
    reshape x1, local copies, waits for them, and re-layouts, build_table(): flattened.reshape(lead + (segments, width, 2 * width - 2))[..., :width]  58.2 us
    dot_general x32, matrix products, one_block(): lax.dot_general(piece, folded, (((2, 3), (1, 2)), ((), ())), preferred_el...  52.2 us
    reduce_scatter x1, waiting for transfers between devices, local(): lax.psum_scatter(correlate(block_rows * lax.axis_size('tm'), table, 0, wh...  43 us
    another operation x2, local copies, waits for them, and re-layouts, build_table(): repeated = jnp.tile(diagonal_line, (1,) * (len(lead) + 1) + (width,))  34.1 us
    dynamic_update_slice x64, local copies, waits for them, and re-layouts, correlate(): lax.map(one_block, jnp.arange(row_count // width, dtype=jnp.int32))  23.2 us
    another operation x1, loops' own time, correlate(): lax.map(one_block, jnp.arange(row_count // width, dtype=jnp.int32))  22.4 us
    dynamic_slice x32, local copies, waits for them, and re-layouts, correlate(): lax.map(one_block, jnp.arange(row_count // width, dtype=jnp.int32))  19 us
    slice x1, local copies, waits for them, and re-layouts, build_table(): lax.slice_in_dim(repeated, width - 1, width - 1 + width * (2 * width - 2)...  15.3 us
  transfers between devices with their start and end apart: 12, of which 5 were waited for; matrix products, arithmetic and copies ran while one was open for 0% of the time, Pallas kernels for 0%

commit v1 on v0

v1 whole, which is shorter than its diff:
```python
import functools
import math

import jax
import jax.numpy as jnp
from jax import lax
from jax.experimental import pallas as pl
from jax.experimental.pallas import tpu as pltpu
from jax.sharding import PartitionSpec as P

SOURCES = 4
MAX_LAG = 512
ROUNDS = 4
LAGS = 1024
WIDTH = 128

epsilon = 1e-06


def swap(block, axis, key):
    count = lax.axis_size(axis)
    return lax.ppermute(block, axis, [(i, i ^ key) for i in range(count)])


def place(base, step, index):
    return pl.multiple_of(base + step * index, 128)


def fill_shifts(line, shifts, round_index):
    length = line.shape[1]
    shape = (WIDTH, 128)
    mask = lax.broadcasted_iota(jnp.int32, shape, 1) >= lax.broadcasted_iota(jnp.int32, shape, 0)
    rows = pl.ds(round_index * WIDTH, WIDTH)

    def body(q, before):
        piece = line[round_index : round_index + 1, pl.ds(place(0, 128, q), 128)]
        now = pltpu.roll(jnp.broadcast_to(piece, shape), 0, 1, stride=1, stride_axis=0)
        shifts[rows, pl.ds(place(0, 128, q), 128)] = jnp.where(mask, now, before).astype(jnp.bfloat16)
        return now

    last = lax.fori_loop(0, length // 128, body, jnp.zeros(shape, jnp.float32), unroll=4)
    shifts[rows, length : length + 128] = jnp.where(mask, 0.0, last).astype(jnp.bfloat16)


def kernel(tiles, groups, plan, *refs):
    strain, mates = refs[:tiles], refs[tiles : tiles + groups]
    out, wide, mate, line, shifts, stacked, total, turned, mate_scale = refs[tiles + groups :]
    channels, tile_len = strain[0].shape
    length = tiles * tile_len
    depth = length + WIDTH
    row_count = out.shape[0]
    blocks = row_count // WIDTH
    here = lax.axis_index("tm")
    low_lag = 0 if row_count == LAGS else lax.rem(here * row_count, LAGS)

    wide[:, :MAX_LAG] = jnp.zeros((channels, MAX_LAG), jnp.bfloat16)
    wide[:, MAX_LAG + length :] = jnp.zeros((channels, MAX_LAG + WIDTH), jnp.bfloat16)
    squares = jnp.zeros((channels, 1), jnp.float32)
    for k in range(tiles):
        wide[:, pl.ds(place(MAX_LAG, tile_len, here ^ k), tile_len)] = strain[k][...]
        widened = strain[k][...].astype(jnp.float32)
        squares += jnp.sum(widened * widened, axis=1, keepdims=True)
        for g in range(groups):
            mate[2 * g : 2 * g + 2, pl.ds(place(0, tile_len, here ^ k), tile_len)] = mates[g][
                :, k * tile_len : (k + 1) * tile_len
            ].astype(jnp.float32)
    scale = lax.rsqrt(squares / length + epsilon) * (1.0 / math.sqrt(length))
    squares = jnp.sum(mate[...] * mate[...], axis=1, keepdims=True)
    mate_scale[...] = jnp.broadcast_to(lax.rsqrt(squares / length + epsilon), mate_scale.shape)

    for r in range(ROUNDS):
        line[r : r + 1, :] = mate[pl.ds(plan[r], 1), :]
        fill_shifts(line, shifts, r)
    for j in range(blocks):
        stacked[channels * j : channels * (j + 1), :] = wide[
            :, pl.ds(place(WIDTH * j, 1, low_lag), depth)
        ]
    total[...] = lax.dot_general(
        stacked[...], shifts[...], (((1,), (1,)), ((), ())), preferred_element_type=jnp.float32
    )
    for j in range(blocks):
        for r in range(ROUNDS):
            both = scale * mate_scale[pl.ds(plan[r], 1), :]
            turned[j % 2, pl.ds(r, channels, stride=ROUNDS), :] = (
                total[channels * j : channels * (j + 1), WIDTH * r : WIDTH * (r + 1)] * both
            )
        out[WIDTH * j : WIDTH * (j + 1), :] = turned[j % 2].T


def correlate(plan, strain, mates, row_count):
    tiles, groups = len(strain), len(mates)
    channels, tile_len = strain[0].shape
    length = tiles * tile_len
    depth = length + WIDTH
    stacked_rows = channels * row_count // WIDTH
    in_vmem = pl.BlockSpec(memory_space=pltpu.VMEM)
    return pl.pallas_call(
        functools.partial(kernel, tiles, groups),
        out_shape=jax.ShapeDtypeStruct((row_count, channels * ROUNDS), jnp.float32),
        in_specs=[pl.BlockSpec(memory_space=pltpu.SMEM)] + [in_vmem] * (tiles + groups),
        out_specs=in_vmem,
        scratch_shapes=[
            pltpu.VMEM((channels, length + 2 * MAX_LAG + WIDTH), jnp.bfloat16),
            pltpu.VMEM((2 * groups, length), jnp.float32),
            pltpu.VMEM((8, length), jnp.float32),
            pltpu.VMEM((ROUNDS * WIDTH, depth), jnp.bfloat16),
            pltpu.VMEM((stacked_rows, depth), jnp.bfloat16),
            pltpu.VMEM((stacked_rows, ROUNDS * WIDTH), jnp.float32),
            pltpu.VMEM((2, channels * ROUNDS, WIDTH), jnp.float32),
            pltpu.VMEM((2 * groups, WIDTH), jnp.float32),
        ],
        compiler_params=pltpu.CompilerParams(vmem_limit_bytes=40 * 2**20),
    )(plan, *strain, *mates)


def local(strain, plan):
    tile_count, block_count = lax.axis_size("tm"), lax.axis_size("sta")
    row_count = SOURCES * LAGS // tile_count
    source = lax.axis_index("tm") * row_count // LAGS
    tiles = [strain] + [swap(strain, "tm", k) for k in range(1, tile_count)]
    row = source * (strain.shape[0] // SOURCES)
    own = jnp.concatenate([lax.dynamic_slice_in_dim(tile, row, 1, 0) for tile in tiles], axis=1)
    pair = jnp.concatenate([own, swap(own, "sta", 1)])
    mates = [pair] + [swap(pair, "sta", 2 * g) for g in range(1, block_count // 2)]
    return correlate(plan, tiles, mates, row_count)


def solution(mesh):
    in_specs = (P("sta", "tm"), P())
    out_specs = P("tm", "sta")
    return jax.shard_map(local, mesh=mesh, in_specs=in_specs, out_specs=out_specs, check_vma=False)
```

time: 342 us -> 26.2 us (0.08); the launches traced: 337 us -> 26 us
  local copies, waits for them, and re-layouts: 164 us -> 0.84 us
  matrix products: 52.2 us -> 0 us
  waiting for transfers between devices: 47 us -> 8.81 us
  loops' own time: 22.4 us -> 0 us
  between operations: 21.2 us -> 0.06 us
  blocking collectives: 13.5 us -> 0 us
  Pallas kernels: 0 us -> 6.96 us
  starting transfers between devices: 14.9 us -> 9.24 us
    reshape x4 -> x0, local copies, waits for them, and re-layouts: 58.3 us -> none  [the longest x1 58.2 us: build_table(): flattened.reshape(lead + (segments, width, 2 * width - 2))[..., :width]]
    dot_general x32 -> x0, matrix products: 52.2 us -> none  [one_block(): lax.dot_general(piece, folded, (((2, 3), (1, 2)), ((), ())), preferred_el...]
    reduce_scatter x1 -> x0, waiting for transfers between devices: 43 us -> none  [local(): lax.psum_scatter(correlate(block_rows * lax.axis_size('tm'), table, 0, wh...]
    another operation x2 -> x0, local copies, waits for them, and re-layouts: 34.1 us -> none  [build_table(): repeated = jnp.tile(diagonal_line, (1,) * (len(lead) + 1) + (width,))]
    dynamic_update_slice x64 -> x0, local copies, waits for them, and re-layouts: 23.2 us -> none  [correlate(): lax.map(one_block, jnp.arange(row_count // width, dtype=jnp.int32))]
    another operation x1 -> x0, loops' own time: 22.4 us -> none  [correlate(): lax.map(one_block, jnp.arange(row_count // width, dtype=jnp.int32))]
    dynamic_slice x32 -> x4, local copies, waits for them, and re-layouts: 19 us -> 0.83 us  [local(): lax.dynamic_slice_in_dim(tile, row, 1, 0)]
    slice x5 -> x0, local copies, waits for them, and re-layouts: 16.8 us -> none  [the longest x1 15.3 us: build_table(): lax.slice_in_dim(repeated, width - 1, width - 1 + width * (2 * width - 2)...]
  transfers between devices with their start and end apart: 12 -> 7, of which waited for: 5 -> 6; matrix products, arithmetic and copies ran while one was open for 0% -> 3% of each run, Pallas kernels for 0% -> 0%
where the time goes in v1:
time: 26.2 us; the launch traced here: 26 us
  starting transfers between devices  9.24 us (35%)
  waiting for transfers between devices  8.81 us (34%)
  Pallas kernels  6.96 us (27%)
  local copies, waits for them, and re-layouts  0.84 us (3%)
    ppermute x7, starting transfers between devices, swap(): return lax.ppermute(block, axis, [(i, i ^ key) for i in range(count)])  9.24 us
    ppermute x7, waiting for transfers between devices, swap(): return lax.ppermute(block, axis, [(i, i ^ key) for i in range(count)])  8.81 us
    pallas_call x1, Pallas kernels, correlate(): pl.pallas_call(functools.partial(kernel, tiles, groups), out_shape=jax.Sh...  6.96 us
    dynamic_slice x4, local copies, waits for them, and re-layouts, local(): lax.dynamic_slice_in_dim(tile, row, 1, 0)  0.83 us
  transfers between devices with their start and end apart: 7, of which 6 were waited for; matrix products, arithmetic and copies ran while one was open for 3% of the time, Pallas kernels for 0%

profile of v1, /device:TPU:0, one launch (start us, length us, event | category | flops | bytes accessed | tf_op | source)
XLA Modules:
  0.0 26.0 jit_solution(5164770544331463178)
XLA Ops:
  0.0 5.0 %collective-permute-start.2 = (bf16[32,1024]{1,0:T(8,128)(2,1)}, bf16[32,1024]{1,0:T(8,128)(2,1)S(1)}, u32[]{:S(2)}, u32[]{:S(2)}) collective-permute-start(bf16[32,1024]{1,0:T(8,128)(2,1)} %refs_0_.1), channel_id=1, source_target_pairs={{0,3},{1,2},{2,1},{3,0},{4,7},{5,6},{6,5},{7,4},{8,11},{9,10},{10,... | collective-permute-start | bytes 196616 | tf_op jit(solution)/shard_map/ppermute | solution.py:22
  5.0 0.0 collective-permute-start.1
  5.1 0.6 %collective-permute-start = (bf16[32,1024]{1,0:T(8,128)(2,1)}, bf16[32,1024]{1,0:T(8,128)(2,1)S(1)}, u32[]{:S(2)}, u32[]{:S(2)}) collective-permute-start(bf16[32,1024]{1,0:T(8,128)(2,1)} %refs_0_.1), channel_id=1, source_target_pairs={{0,1},{1,0},{2,3},{3,2},{4,5},{5,4},{6,7},{7,6},{8,9},{9,8},{10,11... | collective-permute-start | bytes 196616 | tf_op jit(solution)/shard_map/ppermute | solution.py:22
  5.6 0.0 copy-start
  5.6 0.8 %constant_dynamic-slice_fusion.3 = bf16[1,1024]{1,0:T(2,128)(2,1)S(1)} fusion(bf16[32,1024]{1,0:T(8,128)(2,1)} %refs_0_.1, s32[]{:T(128)S(6)} %select_n.12), kind=kLoop, calls=%fused_computation.5 | loop fusion | bytes 4100 | tf_op jit(solution)/shard_map/dynamic_slice | solution.py:122
  6.4 1.5 %collective-permute-done.2.refs_3_ = bf16[32,1024]{1,0:T(8,128)(2,1)S(1)} collective-permute-done((bf16[32,1024]{1,0:T(8,128)(2,1)}, bf16[32,1024]{1,0:T(8,128)(2,1)S(1)}, u32[]{:S(2)}, u32[]{:S(2)}) %collective-permute-start.2) | collective-permute-done | bytes 65568 | tf_op jit(solution)/shard_map/ppermute | solution.py:22
  7.9 3.0 %collective-permute-done.1.refs_2_ = bf16[32,1024]{1,0:T(8,128)(2,1)S(1)} collective-permute-done((bf16[32,1024]{1,0:T(8,128)(2,1)}, bf16[32,1024]{1,0:T(8,128)(2,1)S(1)}, u32[]{:S(2)}, u32[]{:S(2)}) %collective-permute-start.1) | collective-permute-done | bytes 65568 | tf_op jit(solution)/shard_map/ppermute | solution.py:22
  10.9 0.0 collective-permute-done.refs_1_
  10.9 0.0 copy-start.1
  11.0 0.1 collective-permute-start.3
  11.0 1.2 %collective-permute-done.3 = bf16[1,4096]{1,0:T(2,128)(2,1)S(1)} collective-permute-done((bf16[1,4096]{1,0:T(2,128)(2,1)S(1)}, bf16[1,4096]{1,0:T(2,128)(2,1)S(1)}, u32[]{:S(2)}, u32[]{:S(2)}) %collective-permute-start.3) | collective-permute-done | bytes 8224 | tf_op jit(solution)/shard_map/ppermute | solution.py:22
  12.2 2.5 %collective-permute-start.6 = (bf16[2,4096]{1,0:T(2,128)(2,1)S(1)}, bf16[2,4096]{1,0:T(2,128)(2,1)S(1)}, u32[]{:S(2)}, u32[]{:S(2)}) collective-permute-start(bf16[2,4096]{1,0:T(2,128)(2,1)S(1)} %pad_maximum_fusion.1.refs_4_), channel_id=1, source_target_pairs={{0,24},{4,28},{8,16},{12,20},{16,8},{20,12},{24,0},{28,4},{1,25},{... | collective-permute-start | bytes 49160 | tf_op jit(solution)/shard_map/ppermute | solution.py:22
  14.8 0.5 %collective-permute-start.5 = (bf16[2,4096]{1,0:T(2,128)(2,1)S(1)}, bf16[2,4096]{1,0:T(2,128)(2,1)S(1)}, u32[]{:S(2)}, u32[]{:S(2)}) collective-permute-start(bf16[2,4096]{1,0:T(2,128)(2,1)S(1)} %pad_maximum_fusion.1.refs_4_), channel_id=1, source_target_pairs={{0,16},{4,20},{8,24},{12,28},{16,0},{20,4},{24,8},{28,12},{1,17},{... | collective-permute-start | bytes 49160 | tf_op jit(solution)/shard_map/ppermute | solution.py:22
  15.3 0.5 %collective-permute-start.4 = (bf16[2,4096]{1,0:T(2,128)(2,1)S(1)}, bf16[2,4096]{1,0:T(2,128)(2,1)S(1)}, u32[]{:S(2)}, u32[]{:S(2)}) collective-permute-start(bf16[2,4096]{1,0:T(2,128)(2,1)S(1)} %pad_maximum_fusion.1.refs_4_), channel_id=1, source_target_pairs={{0,8},{4,12},{8,0},{12,4},{16,24},{20,28},{24,16},{28,20},{1,9},{5... | collective-permute-start | bytes 49160 | tf_op jit(solution)/shard_map/ppermute | solution.py:22
  15.8 1.1 %collective-permute-done.6.refs_7_ = bf16[2,4096]{1,0:T(2,128)(2,1)S(1)} collective-permute-done((bf16[2,4096]{1,0:T(2,128)(2,1)S(1)}, bf16[2,4096]{1,0:T(2,128)(2,1)S(1)}, u32[]{:S(2)}, u32[]{:S(2)}) %collective-permute-start.6) | collective-permute-done | bytes 16416 | tf_op jit(solution)/shard_map/ppermute | solution.py:22
  17.0 1.5 %collective-permute-done.5.refs_6_ = bf16[2,4096]{1,0:T(2,128)(2,1)S(1)} collective-permute-done((bf16[2,4096]{1,0:T(2,128)(2,1)S(1)}, bf16[2,4096]{1,0:T(2,128)(2,1)S(1)}, u32[]{:S(2)}, u32[]{:S(2)}) %collective-permute-start.5) | collective-permute-done | bytes 16416 | tf_op jit(solution)/shard_map/ppermute | solution.py:22
  18.5 0.5 %collective-permute-done.4.refs_5_ = bf16[2,4096]{1,0:T(2,128)(2,1)S(1)} collective-permute-done((bf16[2,4096]{1,0:T(2,128)(2,1)S(1)}, bf16[2,4096]{1,0:T(2,128)(2,1)S(1)}, u32[]{:S(2)}, u32[]{:S(2)}) %collective-permute-start.4) | collective-permute-done | bytes 16416 | tf_op jit(solution)/shard_map/ppermute | solution.py:22
  19.0 0.0 copy-done
  19.0 0.0 copy-done.1
  19.0 7.0 %shard_map.28 = f32[1024,128]{1,0:T(8,128)} custom-call(s32[4]{0:T(128)S(1)} %copy-done.1, bf16[32,1024]{1,0:T(8,128)(2,1)S(1)} %copy-done, bf16[32,1024]{1,0:T(8,128)(2,1)S(1)} %collective-permute-done.refs_1_, bf16[32,1024]{1,0:T(8,128)(2,1)S(1)} %collective-permute-done.1.refs_2_, bf16[32,1024]{1,0:T(8,128)(2,1)S(1)} %collective-permute-done.2.refs_3_, ...), custom_call_target="tpu_custom_call" | custom-call | tf_op jit(solution)/shard_map/pallas_call | solution.py:97
  (5 shorter events, 0.1 us)
Async XLA Ops:
  0.0 7.9 %collective-permute-start.2 = (bf16[32,1024]{1,0:T(8,128)(2,1)}, bf16[32,1024]{1,0:T(8,128)(2,1)S(1)}, u32[]{:S(2)}, u32[]{:S(2)}) collective-permute-start(bf16[32,1024]{1,0:T(8,128)(2,1)} %refs_0_.1), channel_id=1, source_target_pairs={{0,3},{1,2},{2,1},{3,0},{4,7},{5,6},{6,5},{7,4},{8,11},{9,10},{10,... | collective-permute-start | bytes 196616 | tf_op jit(solution)/shard_map/ppermute | solution.py:22
  5.0 5.8 %collective-permute-start.1 = (bf16[32,1024]{1,0:T(8,128)(2,1)}, bf16[32,1024]{1,0:T(8,128)(2,1)S(1)}, u32[]{:S(2)}, u32[]{:S(2)}) collective-permute-start(bf16[32,1024]{1,0:T(8,128)(2,1)} %refs_0_.1), channel_id=1, source_target_pairs={{0,2},{1,3},{2,0},{3,1},{4,6},{5,7},{6,4},{7,5},{8,10},{9,11},{10,... | collective-permute-start | bytes 196616 | tf_op jit(solution)/shard_map/ppermute | solution.py:22
  5.1 5.8 %collective-permute-start = (bf16[32,1024]{1,0:T(8,128)(2,1)}, bf16[32,1024]{1,0:T(8,128)(2,1)S(1)}, u32[]{:S(2)}, u32[]{:S(2)}) collective-permute-start(bf16[32,1024]{1,0:T(8,128)(2,1)} %refs_0_.1), channel_id=1, source_target_pairs={{0,1},{1,0},{2,3},{3,2},{4,5},{5,4},{6,7},{7,6},{8,9},{9,8},{10,11... | collective-permute-start | bytes 196616 | tf_op jit(solution)/shard_map/ppermute | solution.py:22
  5.6 13.4 %copy-start = (bf16[32,1024]{1,0:T(8,128)(2,1)S(1)}, bf16[32,1024]{1,0:T(8,128)(2,1)}, u32[]{:S(2)}) copy-start(bf16[32,1024]{1,0:T(8,128)(2,1)} %refs_0_.1) | copy-start | bytes 196612
  10.9 8.1 %copy-start.1 = (s32[4]{0:T(128)S(1)}, s32[4]{0:T(128)}, u32[]{:S(2)}) copy-start(s32[4]{0:T(128)} %plan.1) | copy-start | bytes 52
  11.0 1.2 %collective-permute-start.3 = (bf16[1,4096]{1,0:T(2,128)(2,1)S(1)}, bf16[1,4096]{1,0:T(2,128)(2,1)S(1)}, u32[]{:S(2)}, u32[]{:S(2)}) collective-permute-start(bf16[1,4096]{1,0:T(2,128)(2,1)S(1)} %pad_maximum_fusion), channel_id=1, source_target_pairs={{0,4},{4,0},{8,12},{12,8},{16,20},{20,16},{24,28},{28,24},{1,5},{5... | collective-permute-start | bytes 24584 | tf_op jit(solution)/shard_map/ppermute | solution.py:22
  12.2 4.7 %collective-permute-start.6 = (bf16[2,4096]{1,0:T(2,128)(2,1)S(1)}, bf16[2,4096]{1,0:T(2,128)(2,1)S(1)}, u32[]{:S(2)}, u32[]{:S(2)}) collective-permute-start(bf16[2,4096]{1,0:T(2,128)(2,1)S(1)} %pad_maximum_fusion.1.refs_4_), channel_id=1, source_target_pairs={{0,24},{4,28},{8,16},{12,20},{16,8},{20,12},{24,0},{28,4},{1,25},{... | collective-permute-start | bytes 49160 | tf_op jit(solution)/shard_map/ppermute | solution.py:22
  14.8 3.7 %collective-permute-start.5 = (bf16[2,4096]{1,0:T(2,128)(2,1)S(1)}, bf16[2,4096]{1,0:T(2,128)(2,1)S(1)}, u32[]{:S(2)}, u32[]{:S(2)}) collective-permute-start(bf16[2,4096]{1,0:T(2,128)(2,1)S(1)} %pad_maximum_fusion.1.refs_4_), channel_id=1, source_target_pairs={{0,16},{4,20},{8,24},{12,28},{16,0},{20,4},{24,8},{28,12},{1,17},{... | collective-permute-start | bytes 49160 | tf_op jit(solution)/shard_map/ppermute | solution.py:22
  15.3 3.7 %collective-permute-start.4 = (bf16[2,4096]{1,0:T(2,128)(2,1)S(1)}, bf16[2,4096]{1,0:T(2,128)(2,1)S(1)}, u32[]{:S(2)}, u32[]{:S(2)}) collective-permute-start(bf16[2,4096]{1,0:T(2,128)(2,1)S(1)} %pad_maximum_fusion.1.refs_4_), channel_id=1, source_target_pairs={{0,8},{4,12},{8,0},{12,4},{16,24},{20,28},{24,16},{28,20},{1,9},{5... | collective-permute-start | bytes 49160 | tf_op jit(solution)/shard_map/ppermute | solution.py:22

commit v2 on v1

--- a/solution.py
+++ b/solution.py
@@ -23,28 +23,38 @@
 
 
 def place(base, step, index):
+    if isinstance(index, int):
+        return base + step * index
     return pl.multiple_of(base + step * index, 128)
 
 
-def fill_shifts(line, shifts, round_index):
+def fill_shifts(line, shifts):
     length = line.shape[1]
     shape = (WIDTH, 128)
     mask = lax.broadcasted_iota(jnp.int32, shape, 1) >= lax.broadcasted_iota(jnp.int32, shape, 0)
-    rows = pl.ds(round_index * WIDTH, WIDTH)
+    pieces = math.gcd(length // 128, 32)
 
-    def body(q, before):
-        piece = line[round_index : round_index + 1, pl.ds(place(0, 128, q), 128)]
-        now = pltpu.roll(jnp.broadcast_to(piece, shape), 0, 1, stride=1, stride_axis=0)
-        shifts[rows, pl.ds(place(0, 128, q), 128)] = jnp.where(mask, now, before).astype(jnp.bfloat16)
-        return now
+    for r in range(ROUNDS):
+        rows = slice(r * WIDTH, (r + 1) * WIDTH)
 
-    last = lax.fori_loop(0, length // 128, body, jnp.zeros(shape, jnp.float32), unroll=4)
-    shifts[rows, length : length + 128] = jnp.where(mask, 0.0, last).astype(jnp.bfloat16)
+        def body(step, before):
+            for q in range(pieces):
+                at = pl.ds(place(128 * q, 128 * pieces, step), 128)
+                piece = jnp.broadcast_to(line[r : r + 1, at], shape)
+                now = pltpu.roll(piece, 0, 1, stride=1, stride_axis=0)
+                shifts[rows, at] = jnp.where(mask, now, before).astype(jnp.bfloat16)
+                before = now
+            return before
+
+        steps = length // (128 * pieces)
+        zero = jnp.zeros(shape, jnp.float32)
+        last = body(0, zero) if steps == 1 else lax.fori_loop(0, steps, body, zero)
+        shifts[rows, length : length + 128] = jnp.where(mask, 0.0, last).astype(jnp.bfloat16)
 
 
 def kernel(tiles, groups, plan, *refs):
     strain, mates = refs[:tiles], refs[tiles : tiles + groups]
-    out, wide, mate, line, shifts, stacked, total, turned, mate_scale = refs[tiles + groups :]
+    out, wide, mate, line, shifts, stacked, total, turned = refs[tiles + groups :]
     channels, tile_len = strain[0].shape
     length = tiles * tile_len
     depth = length + WIDTH
@@ -57,20 +67,22 @@
     wide[:, MAX_LAG + length :] = jnp.zeros((channels, MAX_LAG + WIDTH), jnp.bfloat16)
     squares = jnp.zeros((channels, 1), jnp.float32)
     for k in range(tiles):
-        wide[:, pl.ds(place(MAX_LAG, tile_len, here ^ k), tile_len)] = strain[k][...]
         widened = strain[k][...].astype(jnp.float32)
         squares += jnp.sum(widened * widened, axis=1, keepdims=True)
         for g in range(groups):
             mate[2 * g : 2 * g + 2, pl.ds(place(0, tile_len, here ^ k), tile_len)] = mates[g][
                 :, k * tile_len : (k + 1) * tile_len
             ].astype(jnp.float32)
-    scale = lax.rsqrt(squares / length + epsilon) * (1.0 / math.sqrt(length))
-    squares = jnp.sum(mate[...] * mate[...], axis=1, keepdims=True)
-    mate_scale[...] = jnp.broadcast_to(lax.rsqrt(squares / length + epsilon), mate_scale.shape)
-
+    scale = lax.rsqrt(squares / length + epsilon)
+    for k in range(tiles):
+        wide[:, pl.ds(place(MAX_LAG, tile_len, here ^ k), tile_len)] = (
+            strain[k][...].astype(jnp.float32) * scale
+        ).astype(jnp.bfloat16)
     for r in range(ROUNDS):
         line[r : r + 1, :] = mate[pl.ds(plan[r], 1), :]
-        fill_shifts(line, shifts, r)
+    squares = jnp.sum(line[...] * line[...], axis=1, keepdims=True)
+    line[...] = (line[...] * lax.rsqrt(squares / length + epsilon)).astype(jnp.bfloat16).astype(jnp.float32)
+    fill_shifts(line, shifts)
     for j in range(blocks):
         stacked[channels * j : channels * (j + 1), :] = wide[
             :, pl.ds(place(WIDTH * j, 1, low_lag), depth)
@@ -80,11 +92,10 @@
     )
     for j in range(blocks):
         for r in range(ROUNDS):
-            both = scale * mate_scale[pl.ds(plan[r], 1), :]
-            turned[j % 2, pl.ds(r, channels, stride=ROUNDS), :] = (
-                total[channels * j : channels * (j + 1), WIDTH * r : WIDTH * (r + 1)] * both
-            )
-        out[WIDTH * j : WIDTH * (j + 1), :] = turned[j % 2].T
+            turned[j % 2, pl.ds(r, channels, stride=ROUNDS), :] = total[
+                channels * j : channels * (j + 1), WIDTH * r : WIDTH * (r + 1)
+            ]
+        out[WIDTH * j : WIDTH * (j + 1), :] = turned[j % 2].T * (1.0 / math.sqrt(length))
 
 
 def correlate(plan, strain, mates, row_count):
@@ -102,12 +113,11 @@
         scratch_shapes=[
             pltpu.VMEM((channels, length + 2 * MAX_LAG + WIDTH), jnp.bfloat16),
             pltpu.VMEM((2 * groups, length), jnp.float32),
-            pltpu.VMEM((8, length), jnp.float32),
+            pltpu.VMEM((ROUNDS, length), jnp.float32),
             pltpu.VMEM((ROUNDS * WIDTH, depth), jnp.bfloat16),
             pltpu.VMEM((stacked_rows, depth), jnp.bfloat16),
             pltpu.VMEM((stacked_rows, ROUNDS * WIDTH), jnp.float32),
             pltpu.VMEM((2, channels * ROUNDS, WIDTH), jnp.float32),
-            pltpu.VMEM((2 * groups, WIDTH), jnp.float32),
         ],
         compiler_params=pltpu.CompilerParams(vmem_limit_bytes=40 * 2**20),
     )(plan, *strain, *mates)

time: 26.2 us -> 23 us (0.88)
  Pallas kernels: 6.96 us -> 3.79 us
    pallas_call x1, Pallas kernels: 6.96 us -> 3.79 us  [correlate(): pl.pallas_call(functools.partial(kernel, tiles, groups), out_shape=jax.Sh...]
  transfers between devices with their start and end apart: 7 -> 7, of which waited for: 6 -> 6; matrix products, arithmetic and copies ran while one was open for 3% -> 4% of each run, Pallas kernels for 0% -> 0%
where the time goes in v2:
time: 23 us; the launch traced here: 22.8 us
  starting transfers between devices  9.24 us (40%)
  waiting for transfers between devices  8.81 us (38%)
  Pallas kernels  3.79 us (16%)
  local copies, waits for them, and re-layouts  0.84 us (4%)
    ppermute x7, starting transfers between devices, swap(): return lax.ppermute(block, axis, [(i, i ^ key) for i in range(count)])  9.24 us
    ppermute x7, waiting for transfers between devices, swap(): return lax.ppermute(block, axis, [(i, i ^ key) for i in range(count)])  8.81 us
    pallas_call x1, Pallas kernels, correlate(): pl.pallas_call(functools.partial(kernel, tiles, groups), out_shape=jax.Sh...  3.79 us
    dynamic_slice x4, local copies, waits for them, and re-layouts, local(): lax.dynamic_slice_in_dim(tile, row, 1, 0)  0.83 us
  transfers between devices with their start and end apart: 7, of which 6 were waited for; matrix products, arithmetic and copies ran while one was open for 4% of the time, Pallas kernels for 0%

profile of v2, /device:TPU:0, one launch (start us, length us, event | category | flops | bytes accessed | tf_op | source)
XLA Modules:
  0.0 22.8 jit_solution(3836771631798132007)
XLA Ops:
  0.0 5.0 %collective-permute-start.2 = (bf16[32,1024]{1,0:T(8,128)(2,1)}, bf16[32,1024]{1,0:T(8,128)(2,1)S(1)}, u32[]{:S(2)}, u32[]{:S(2)}) collective-permute-start(bf16[32,1024]{1,0:T(8,128)(2,1)} %refs_0_.1), channel_id=1, source_target_pairs={{0,3},{1,2},{2,1},{3,0},{4,7},{5,6},{6,5},{7,4},{8,11},{9,10},{10,... | collective-permute-start | bytes 196616 | tf_op jit(solution)/shard_map/ppermute | solution.py:22
  5.0 0.0 collective-permute-start.1
  5.1 0.6 %collective-permute-start = (bf16[32,1024]{1,0:T(8,128)(2,1)}, bf16[32,1024]{1,0:T(8,128)(2,1)S(1)}, u32[]{:S(2)}, u32[]{:S(2)}) collective-permute-start(bf16[32,1024]{1,0:T(8,128)(2,1)} %refs_0_.1), channel_id=1, source_target_pairs={{0,1},{1,0},{2,3},{3,2},{4,5},{5,4},{6,7},{7,6},{8,9},{9,8},{10,11... | collective-permute-start | bytes 196616 | tf_op jit(solution)/shard_map/ppermute | solution.py:22
  5.6 0.0 copy-start
  5.6 0.8 %constant_dynamic-slice_fusion.3 = bf16[1,1024]{1,0:T(2,128)(2,1)S(1)} fusion(bf16[32,1024]{1,0:T(8,128)(2,1)} %refs_0_.1, s32[]{:T(128)S(6)} %select_n.12), kind=kLoop, calls=%fused_computation.5 | loop fusion | bytes 4100 | tf_op jit(solution)/shard_map/dynamic_slice | solution.py:132
  6.4 1.5 %collective-permute-done.2.refs_3_ = bf16[32,1024]{1,0:T(8,128)(2,1)S(1)} collective-permute-done((bf16[32,1024]{1,0:T(8,128)(2,1)}, bf16[32,1024]{1,0:T(8,128)(2,1)S(1)}, u32[]{:S(2)}, u32[]{:S(2)}) %collective-permute-start.2) | collective-permute-done | bytes 65568 | tf_op jit(solution)/shard_map/ppermute | solution.py:22
  7.9 3.0 %collective-permute-done.1.refs_2_ = bf16[32,1024]{1,0:T(8,128)(2,1)S(1)} collective-permute-done((bf16[32,1024]{1,0:T(8,128)(2,1)}, bf16[32,1024]{1,0:T(8,128)(2,1)S(1)}, u32[]{:S(2)}, u32[]{:S(2)}) %collective-permute-start.1) | collective-permute-done | bytes 65568 | tf_op jit(solution)/shard_map/ppermute | solution.py:22
  10.9 0.0 collective-permute-done.refs_1_
  10.9 0.0 copy-start.1
  11.0 0.1 collective-permute-start.3
  11.0 1.2 %collective-permute-done.3 = bf16[1,4096]{1,0:T(2,128)(2,1)S(1)} collective-permute-done((bf16[1,4096]{1,0:T(2,128)(2,1)S(1)}, bf16[1,4096]{1,0:T(2,128)(2,1)S(1)}, u32[]{:S(2)}, u32[]{:S(2)}) %collective-permute-start.3) | collective-permute-done | bytes 8224 | tf_op jit(solution)/shard_map/ppermute | solution.py:22
  12.2 2.5 %collective-permute-start.6 = (bf16[2,4096]{1,0:T(2,128)(2,1)S(1)}, bf16[2,4096]{1,0:T(2,128)(2,1)S(1)}, u32[]{:S(2)}, u32[]{:S(2)}) collective-permute-start(bf16[2,4096]{1,0:T(2,128)(2,1)S(1)} %pad_maximum_fusion.1.refs_4_), channel_id=1, source_target_pairs={{0,24},{4,28},{8,16},{12,20},{16,8},{20,12},{24,0},{28,4},{1,25},{... | collective-permute-start | bytes 49160 | tf_op jit(solution)/shard_map/ppermute | solution.py:22
  14.8 0.5 %collective-permute-start.5 = (bf16[2,4096]{1,0:T(2,128)(2,1)S(1)}, bf16[2,4096]{1,0:T(2,128)(2,1)S(1)}, u32[]{:S(2)}, u32[]{:S(2)}) collective-permute-start(bf16[2,4096]{1,0:T(2,128)(2,1)S(1)} %pad_maximum_fusion.1.refs_4_), channel_id=1, source_target_pairs={{0,16},{4,20},{8,24},{12,28},{16,0},{20,4},{24,8},{28,12},{1,17},{... | collective-permute-start | bytes 49160 | tf_op jit(solution)/shard_map/ppermute | solution.py:22
  15.3 0.5 %collective-permute-start.4 = (bf16[2,4096]{1,0:T(2,128)(2,1)S(1)}, bf16[2,4096]{1,0:T(2,128)(2,1)S(1)}, u32[]{:S(2)}, u32[]{:S(2)}) collective-permute-start(bf16[2,4096]{1,0:T(2,128)(2,1)S(1)} %pad_maximum_fusion.1.refs_4_), channel_id=1, source_target_pairs={{0,8},{4,12},{8,0},{12,4},{16,24},{20,28},{24,16},{28,20},{1,9},{5... | collective-permute-start | bytes 49160 | tf_op jit(solution)/shard_map/ppermute | solution.py:22
  15.8 1.1 %collective-permute-done.6.refs_7_ = bf16[2,4096]{1,0:T(2,128)(2,1)S(1)} collective-permute-done((bf16[2,4096]{1,0:T(2,128)(2,1)S(1)}, bf16[2,4096]{1,0:T(2,128)(2,1)S(1)}, u32[]{:S(2)}, u32[]{:S(2)}) %collective-permute-start.6) | collective-permute-done | bytes 16416 | tf_op jit(solution)/shard_map/ppermute | solution.py:22
  17.0 1.5 %collective-permute-done.5.refs_6_ = bf16[2,4096]{1,0:T(2,128)(2,1)S(1)} collective-permute-done((bf16[2,4096]{1,0:T(2,128)(2,1)S(1)}, bf16[2,4096]{1,0:T(2,128)(2,1)S(1)}, u32[]{:S(2)}, u32[]{:S(2)}) %collective-permute-start.5) | collective-permute-done | bytes 16416 | tf_op jit(solution)/shard_map/ppermute | solution.py:22
  18.5 0.5 %collective-permute-done.4.refs_5_ = bf16[2,4096]{1,0:T(2,128)(2,1)S(1)} collective-permute-done((bf16[2,4096]{1,0:T(2,128)(2,1)S(1)}, bf16[2,4096]{1,0:T(2,128)(2,1)S(1)}, u32[]{:S(2)}, u32[]{:S(2)}) %collective-permute-start.4) | collective-permute-done | bytes 16416 | tf_op jit(solution)/shard_map/ppermute | solution.py:22
  19.0 0.0 copy-done
  19.0 0.0 copy-done.1
  19.0 3.8 %shard_map.28 = f32[1024,128]{1,0:T(8,128)} custom-call(s32[4]{0:T(128)S(1)} %copy-done.1, bf16[32,1024]{1,0:T(8,128)(2,1)S(1)} %copy-done, bf16[32,1024]{1,0:T(8,128)(2,1)S(1)} %collective-permute-done.refs_1_, bf16[32,1024]{1,0:T(8,128)(2,1)S(1)} %collective-permute-done.1.refs_2_, bf16[32,1024]{1,0:T(8,128)(2,1)S(1)} %collective-permute-done.2.refs_3_, ...), custom_call_target="tpu_custom_call" | custom-call | tf_op jit(solution)/shard_map/pallas_call | solution.py:108
  (5 shorter events, 0.1 us)
Async XLA Ops:
  0.0 7.9 %collective-permute-start.2 = (bf16[32,1024]{1,0:T(8,128)(2,1)}, bf16[32,1024]{1,0:T(8,128)(2,1)S(1)}, u32[]{:S(2)}, u32[]{:S(2)}) collective-permute-start(bf16[32,1024]{1,0:T(8,128)(2,1)} %refs_0_.1), channel_id=1, source_target_pairs={{0,3},{1,2},{2,1},{3,0},{4,7},{5,6},{6,5},{7,4},{8,11},{9,10},{10,... | collective-permute-start | bytes 196616 | tf_op jit(solution)/shard_map/ppermute | solution.py:22
  5.0 5.8 %collective-permute-start.1 = (bf16[32,1024]{1,0:T(8,128)(2,1)}, bf16[32,1024]{1,0:T(8,128)(2,1)S(1)}, u32[]{:S(2)}, u32[]{:S(2)}) collective-permute-start(bf16[32,1024]{1,0:T(8,128)(2,1)} %refs_0_.1), channel_id=1, source_target_pairs={{0,2},{1,3},{2,0},{3,1},{4,6},{5,7},{6,4},{7,5},{8,10},{9,11},{10,... | collective-permute-start | bytes 196616 | tf_op jit(solution)/shard_map/ppermute | solution.py:22
  5.1 5.8 %collective-permute-start = (bf16[32,1024]{1,0:T(8,128)(2,1)}, bf16[32,1024]{1,0:T(8,128)(2,1)S(1)}, u32[]{:S(2)}, u32[]{:S(2)}) collective-permute-start(bf16[32,1024]{1,0:T(8,128)(2,1)} %refs_0_.1), channel_id=1, source_target_pairs={{0,1},{1,0},{2,3},{3,2},{4,5},{5,4},{6,7},{7,6},{8,9},{9,8},{10,11... | collective-permute-start | bytes 196616 | tf_op jit(solution)/shard_map/ppermute | solution.py:22
  5.6 13.4 %copy-start = (bf16[32,1024]{1,0:T(8,128)(2,1)S(1)}, bf16[32,1024]{1,0:T(8,128)(2,1)}, u32[]{:S(2)}) copy-start(bf16[32,1024]{1,0:T(8,128)(2,1)} %refs_0_.1) | copy-start | bytes 196612
  10.9 8.1 %copy-start.1 = (s32[4]{0:T(128)S(1)}, s32[4]{0:T(128)}, u32[]{:S(2)}) copy-start(s32[4]{0:T(128)} %plan.1) | copy-start | bytes 52
  11.0 1.2 %collective-permute-start.3 = (bf16[1,4096]{1,0:T(2,128)(2,1)S(1)}, bf16[1,4096]{1,0:T(2,128)(2,1)S(1)}, u32[]{:S(2)}, u32[]{:S(2)}) collective-permute-start(bf16[1,4096]{1,0:T(2,128)(2,1)S(1)} %pad_maximum_fusion), channel_id=1, source_target_pairs={{0,4},{4,0},{8,12},{12,8},{16,20},{20,16},{24,28},{28,24},{1,5},{5... | collective-permute-start | bytes 24584 | tf_op jit(solution)/shard_map/ppermute | solution.py:22
  12.2 4.7 %collective-permute-start.6 = (bf16[2,4096]{1,0:T(2,128)(2,1)S(1)}, bf16[2,4096]{1,0:T(2,128)(2,1)S(1)}, u32[]{:S(2)}, u32[]{:S(2)}) collective-permute-start(bf16[2,4096]{1,0:T(2,128)(2,1)S(1)} %pad_maximum_fusion.1.refs_4_), channel_id=1, source_target_pairs={{0,24},{4,28},{8,16},{12,20},{16,8},{20,12},{24,0},{28,4},{1,25},{... | collective-permute-start | bytes 49160 | tf_op jit(solution)/shard_map/ppermute | solution.py:22
  14.8 3.7 %collective-permute-start.5 = (bf16[2,4096]{1,0:T(2,128)(2,1)S(1)}, bf16[2,4096]{1,0:T(2,128)(2,1)S(1)}, u32[]{:S(2)}, u32[]{:S(2)}) collective-permute-start(bf16[2,4096]{1,0:T(2,128)(2,1)S(1)} %pad_maximum_fusion.1.refs_4_), channel_id=1, source_target_pairs={{0,16},{4,20},{8,24},{12,28},{16,0},{20,4},{24,8},{28,12},{1,17},{... | collective-permute-start | bytes 49160 | tf_op jit(solution)/shard_map/ppermute | solution.py:22
  15.3 3.7 %collective-permute-start.4 = (bf16[2,4096]{1,0:T(2,128)(2,1)S(1)}, bf16[2,4096]{1,0:T(2,128)(2,1)S(1)}, u32[]{:S(2)}, u32[]{:S(2)}) collective-permute-start(bf16[2,4096]{1,0:T(2,128)(2,1)S(1)} %pad_maximum_fusion.1.refs_4_), channel_id=1, source_target_pairs={{0,8},{4,12},{8,0},{12,4},{16,24},{20,28},{24,16},{28,20},{1,9},{5... | collective-permute-start | bytes 49160 | tf_op jit(solution)/shard_map/ppermute | solution.py:22

commit v3 on v2

v3 whole, which is shorter than its diff:
```python
import functools
import itertools
import math

import jax
import jax.numpy as jnp
from jax import lax
from jax.experimental import pallas as pl
from jax.experimental.pallas import tpu as pltpu
from jax.sharding import PartitionSpec as P

SOURCES = 4
MAX_LAG = 512
ROUNDS = 4
LAGS = 1024
WIDTH = 64
HALVES = 128 // WIDTH
MOST_BRANCHES = 16

epsilon = 1e-06


def swap(block, axis, key):
    count = lax.axis_size(axis)
    return lax.ppermute(block, axis, [(i, i ^ key) for i in range(count)])


def place(base, step, index):
    if isinstance(index, int):
        return base + step * index
    return pl.multiple_of(base + step * index, 128)


def stack_strain(keys, strain, stacked, wide):
    channels, tile_len = strain[0].shape
    length = len(keys) * tile_len
    blocks = stacked.shape[0] // channels
    here = lax.axis_index("tm")
    row_count = blocks * WIDTH
    low_lag = 0 if row_count == LAGS else lax.rem(here * row_count, LAGS)

    wide[0][:, :MAX_LAG] = jnp.zeros((channels, MAX_LAG), jnp.bfloat16)
    wide[0][:, MAX_LAG + length :] = jnp.zeros((channels, MAX_LAG + 128), jnp.bfloat16)
    squares = jnp.zeros((channels, 1), jnp.float32)
    for tile in strain:
        widened = tile[...].astype(jnp.float32)
        squares += jnp.sum(widened * widened, axis=1, keepdims=True)
    scale = lax.rsqrt(squares / length + epsilon)
    for key, tile in zip(keys, strain):
        wide[0][:, pl.ds(place(MAX_LAG, tile_len, here ^ key), tile_len)] = (
            tile[...].astype(jnp.float32) * scale
        ).astype(jnp.bfloat16)
    for half in range(1, HALVES):
        kept = wide[half].shape[1]
        wide[half][...] = wide[0][:, WIDTH * half : WIDTH * half + kept]
    for j in range(blocks):
        stacked[channels * j : channels * (j + 1), :] = wide[j % HALVES][
            :, pl.ds(place(128 * (j // HALVES), 1, low_lag), stacked.shape[1])
        ]


def fill_shifts(line, shifts):
    length = line.shape[1]
    shape = (WIDTH, 128)
    mask = lax.broadcasted_iota(jnp.int32, shape, 1) >= lax.broadcasted_iota(jnp.int32, shape, 0)
    pieces = math.gcd(length // 128, 32)

    for r in range(ROUNDS):
        rows = slice(r * WIDTH, (r + 1) * WIDTH)

        def body(step, before):
            for q in range(pieces):
                at = pl.ds(place(128 * q, 128 * pieces, step), 128)
                piece = jnp.broadcast_to(line[r : r + 1, at], shape)
                now = pltpu.roll(piece, 0, 1, stride=1, stride_axis=0)
                shifts[rows, at] = jnp.where(mask, now, before).astype(jnp.bfloat16)
                before = now
            return before

        steps = length // (128 * pieces)
        zero = jnp.zeros(shape, jnp.float32)
        last = body(0, zero) if steps == 1 else lax.fori_loop(0, steps, body, zero)
        shifts[rows, length : length + 128] = jnp.where(mask, 0.0, last).astype(jnp.bfloat16)


def correlate_kernel(keys, groups, chosen_far, *refs):
    tiles = len(keys)
    strain, far, (out, *refs) = refs[:tiles], refs[tiles : tiles + groups], refs[tiles + groups :]
    mates, refs = refs[:groups], refs[groups:]
    chosen, mate, line, stacked, shifts, total, turned, ready, fetched, sent, *wide = refs
    row_count = out.shape[0]
    channels, tile_len = strain[0].shape
    length = line.shape[1]
    here = lax.axis_index("tm")

    copies = [pltpu.make_async_copy(far[g], mates[g], fetched.at[g]) for g in range(groups)]
    copies.append(pltpu.make_async_copy(chosen_far, chosen, fetched.at[groups]))
    for copy in copies:
        copy.start()
    stack_strain(keys, strain, stacked, wide)
    for copy in copies:
        copy.wait()
    at = 0
    for group in mates:
        count = group.shape[0]
        for k, key in enumerate(keys):
            mate[at : at + count, pl.ds(place(0, tile_len, here ^ key), tile_len)] = group[
                :, k * tile_len : (k + 1) * tile_len
            ].astype(jnp.float32)
        at += count
    for r in range(ROUNDS):
        line[r : r + 1, :] = mate[pl.ds(chosen[r], 1), :]
    squares = jnp.sum(line[...] * line[...], axis=1, keepdims=True)
    whitened = line[...] * lax.rsqrt(squares / length + epsilon)
    line[...] = whitened.astype(jnp.bfloat16).astype(jnp.float32)
    fill_shifts(line, shifts)
    total[...] = lax.dot_general(
        stacked[...], shifts[...], (((1,), (1,)), ((), ())), preferred_element_type=jnp.float32
    )
    copies = []
    lane = lax.broadcasted_iota(jnp.int32, (channels, 128), 1)
    for block in range(row_count // 128):
        for r in range(ROUNDS):
            value = jnp.zeros((channels, 128), jnp.float32)
            for half in range(HALVES):
                rows = slice((block * HALVES + half) * channels, (block * HALVES + half + 1) * channels)
                first = WIDTH * r // 128 * 128
                part = total[rows, first : first + 128]
                if WIDTH * half != WIDTH * r - first:
                    part = pltpu.roll(part, (WIDTH * half - WIDTH * r + first) % 128, 1)
                value = part if half == 0 else jnp.where(lane >= WIDTH * half, part, value)
            turned[block % 2, pl.ds(r, channels, stride=ROUNDS), :] = value
        lags = slice(128 * block, 128 * (block + 1))
        ready[lags, :] = turned[block % 2].T * (1.0 / math.sqrt(length))
        copies.append(pltpu.make_async_copy(ready.at[lags], out.at[lags], sent.at[block]))
        copies[-1].start()
    for copy in copies:
        copy.wait()


def correlate(keys, chosen, strain, mates, row_count):
    channels, tile_len = strain[0].shape
    length = len(keys) * tile_len
    depth = length + 128
    stacked_rows = channels * row_count // WIDTH
    mate_rows = sum(group.shape[0] for group in mates)
    in_vmem = pl.BlockSpec(memory_space=pltpu.VMEM)
    anywhere = pl.BlockSpec(memory_space=pl.ANY)
    widths = [length + 2 * MAX_LAG + 128] + [length + 2 * MAX_LAG] * (HALVES - 1)
    return pl.pallas_call(
        functools.partial(correlate_kernel, keys, len(mates)),
        out_shape=jax.ShapeDtypeStruct((row_count, channels * ROUNDS), jnp.float32),
        in_specs=[anywhere]
        + [in_vmem] * len(strain)
        + [anywhere] * len(mates),
        out_specs=pl.BlockSpec(memory_space=pltpu.HBM),
        scratch_shapes=[
            *(pltpu.VMEM(group.shape, jnp.bfloat16) for group in mates),
            pltpu.SMEM(chosen.shape, jnp.int32),
            pltpu.VMEM((mate_rows, length), jnp.float32),
            pltpu.VMEM((ROUNDS, length), jnp.float32),
            pltpu.VMEM((stacked_rows, depth), jnp.bfloat16),
            pltpu.VMEM((ROUNDS * WIDTH, depth), jnp.bfloat16),
            pltpu.VMEM((stacked_rows, ROUNDS * WIDTH), jnp.float32),
            pltpu.VMEM((2, channels * ROUNDS, 128), jnp.float32),
            pltpu.VMEM((row_count, channels * ROUNDS), jnp.float32),
            pltpu.SemaphoreType.DMA((len(mates) + 1,)),
            pltpu.SemaphoreType.DMA((row_count // 128,)),
            *(pltpu.VMEM((channels, width), jnp.bfloat16) for width in widths),
        ],
        compiler_params=pltpu.CompilerParams(vmem_limit_bytes=40 * 2**20),
    )(chosen, *strain, *mates)


def by_plan(plan, own):
    block_count = lax.axis_size("sta")
    middle = range(2, block_count - 1)
    choices = list(itertools.combinations(middle, ROUNDS - 2))
    ends = (plan == 1) | (plan == block_count - 1)
    high = jnp.max(jnp.where(ends, 0, plan))
    low = jnp.min(jnp.where(ends, block_count, plan))
    first, span = low - 2, 2 * len(middle) - 1
    index = ((first * (span - first)) >> 1) + high - low - 1

    def branch(keys):
        return lambda own: jnp.concatenate([swap(own, "sta", key) for key in keys])

    branches = [branch((1, *keys, block_count - 1)) for keys in choices]
    ranks = jnp.sum((plan[None, :] < plan[:, None]).astype(jnp.int32), axis=1)
    index, ranks = lax.optimization_barrier((index, ranks))
    return ranks, lax.switch(index, branches, own)


def local(strain, plan):
    tile_count, block_count = lax.axis_size("tm"), lax.axis_size("sta")
    row_count = SOURCES * LAGS // tile_count
    source = lax.axis_index("tm") * row_count // LAGS
    order = sorted(range(tile_count), key=lambda k: (k > 1, k if k < 2 else -k))
    tiles = [strain] + [swap(strain, "tm", k) for k in order[1:]]
    row = source * (strain.shape[0] // SOURCES)
    own = jnp.concatenate([lax.dynamic_slice_in_dim(tile, row, 1, 0) for tile in tiles], axis=1)
    if math.comb(max(block_count - 3, 0), ROUNDS - 2) in range(1, MOST_BRANCHES + 1):
        chosen, mates = by_plan(plan, own)
        mates = [mates]
    else:
        chosen = plan
        pair = jnp.concatenate([own, swap(own, "sta", 1)])
        mates = [pair] + [swap(pair, "sta", 2 * g) for g in range(1, block_count // 2)]
    return correlate(order, chosen, tiles, mates, row_count)


def solution(mesh):
    in_specs = (P("sta", "tm"), P())
    out_specs = P("tm", "sta")
    return jax.shard_map(local, mesh=mesh, in_specs=in_specs, out_specs=out_specs, check_vma=False)
```

time: 23 us -> 20.4 us (0.89); the launches traced: 22.8 us -> 20.6 us
  waiting for transfers between devices: 8.81 us -> 2.98 us
  other arithmetic: 0.06 us -> 2.38 us
  between operations: 0.06 us -> 2.08 us
  local copies, waits for them, and re-layouts: 0.84 us -> 0.05 us
  Pallas kernels: 3.79 us -> 3.33 us
  starting transfers between devices: 9.24 us -> 9.68 us
    ppermute x7, waiting for transfers between devices: 8.81 us -> 2.98 us  [swap(): return lax.ppermute(block, axis, [(i, i ^ key) for i in range(count)])]
    reduce_max x0 -> x1, other arithmetic: none -> 1.36 us  [by_plan(): high = jnp.max(jnp.where(ends, 0, plan))]
    reduce_sum x0 -> x1, other arithmetic: none -> 0.91 us  [by_plan(): ranks = jnp.sum((plan[None, :] < plan[:, None]).astype(jnp.int32), axis=1)]
    dynamic_slice x4, local copies, waits for them, and re-layouts: 0.83 us -> 0.05 us  [local(): lax.dynamic_slice_in_dim(tile, row, 1, 0)]
    pallas_call x1, Pallas kernels: 3.79 us -> 3.33 us  [correlate(): pl.pallas_call(functools.partial(correlate_kernel, keys, len(mates)), out...]
    ppermute x7, starting transfers between devices: 9.24 us -> 9.68 us  [swap(): return lax.ppermute(block, axis, [(i, i ^ key) for i in range(count)])]
  transfers between devices with their start and end apart: 7 -> 7, of which waited for: 6 -> 5; matrix products, arithmetic and copies ran while one was open for 4% -> 11% of each run, Pallas kernels for 0% -> 0%
where the time goes in v3:
time: 20.4 us; the launch traced here: 20.6 us
  starting transfers between devices  9.68 us (47%)
  Pallas kernels  3.33 us (16%)
  waiting for transfers between devices  2.98 us (15%)
  other arithmetic  2.38 us (12%)
  between operations  2.08 us (10%)
    ppermute x7, starting transfers between devices, swap(): return lax.ppermute(block, axis, [(i, i ^ key) for i in range(count)])  9.68 us
    pallas_call x1, Pallas kernels, correlate(): pl.pallas_call(functools.partial(correlate_kernel, keys, len(mates)), out...  3.33 us
    ppermute x7, waiting for transfers between devices, swap(): return lax.ppermute(block, axis, [(i, i ^ key) for i in range(count)])  2.98 us
    reduce_max x1, other arithmetic, by_plan(): high = jnp.max(jnp.where(ends, 0, plan))  1.36 us
    reduce_sum x1, other arithmetic, by_plan(): ranks = jnp.sum((plan[None, :] < plan[:, None]).astype(jnp.int32), axis=1)  0.91 us
  transfers between devices with their start and end apart: 7, of which 5 were waited for; matrix products, arithmetic and copies ran while one was open for 11% of the time, Pallas kernels for 0%

profile of v3, /device:TPU:0, one launch (start us, length us, event | category | flops | bytes accessed | tf_op | source)
XLA Modules:
  0.0 20.6 jit_solution(17177737848382897957)
XLA Ops:
  0.0 0.0 copy-start
  0.0 4.0 %collective-permute-start.42 = (bf16[32,1024]{1,0:T(8,128)(2,1)}, bf16[32,1024]{1,0:T(8,128)(2,1)S(1)}, u32[]{:S(2)}, u32[]{:S(2)}) collective-permute-start(bf16[32,1024]{1,0:T(8,128)(2,1)} %refs_0_.1), channel_id=1, source_target_pairs={{0,2},{1,3},{2,0},{3,1},{4,6},{5,7},{6,4},{7,5},{8,10},{9,11},{10,... | collective-permute-start | bytes 196616 | tf_op jit(solution)/shard_map/ppermute | solution.py:25
  4.0 1.3 %collective-permute-start.41 = (bf16[32,1024]{1,0:T(8,128)(2,1)}, bf16[32,1024]{1,0:T(8,128)(2,1)S(1)}, u32[]{:S(2)}, u32[]{:S(2)}) collective-permute-start(bf16[32,1024]{1,0:T(8,128)(2,1)} %refs_0_.1), channel_id=1, source_target_pairs={{0,3},{1,2},{2,1},{3,0},{4,7},{5,6},{6,5},{7,4},{8,11},{9,10},{10,... | collective-permute-start | bytes 196616 | tf_op jit(solution)/shard_map/ppermute | solution.py:25
  5.4 0.2 %collective-permute-start.40 = (bf16[32,1024]{1,0:T(8,128)(2,1)}, bf16[32,1024]{1,0:T(8,128)(2,1)S(1)}, u32[]{:S(2)}, u32[]{:S(2)}) collective-permute-start(bf16[32,1024]{1,0:T(8,128)(2,1)} %refs_0_.1), channel_id=1, source_target_pairs={{0,1},{1,0},{2,3},{3,2},{4,5},{5,4},{6,7},{7,6},{8,9},{9,8},{10,11... | collective-permute-start | bytes 196616 | tf_op jit(solution)/shard_map/ppermute | solution.py:25
  5.6 0.9 %convert_reduce_fusion.chosen_far = s32[4]{0:T(128)S(1)} fusion(s32[4]{0:T(128)} %param.13), kind=kLoop, calls=%fused_computation.11 | loop fusion | flops 44 | bytes 32 | tf_op jit(solution)/shard_map/reduce_sum | solution.py:189
  6.5 1.4 %fusion.3 = (s32[]{:T(128)}, s32[]{:T(128)}) fusion(s32[4]{0:T(128)} %param.13), kind=kLoop, calls=%fused_computation.20 | loop fusion | flops 26 | bytes 24 | tf_op jit(solution)/shard_map/reduce_max | solution.py:180
  9.9 0.0 copy-done
  9.9 0.0 collective-permute-done.42.refs_3_
  10.0 0.5 %collective-permute-done.41.refs_2_ = bf16[32,1024]{1,0:T(8,128)(2,1)S(1)} collective-permute-done((bf16[32,1024]{1,0:T(8,128)(2,1)}, bf16[32,1024]{1,0:T(8,128)(2,1)S(1)}, u32[]{:S(2)}, u32[]{:S(2)}) %collective-permute-start.41) | collective-permute-done | bytes 65568 | tf_op jit(solution)/shard_map/ppermute | solution.py:25
  10.5 0.1 collective-permute-done.40.refs_1_
  10.6 6.6 %conditional.1 = (bf16[4,4096]{1,0:T(4,128)(2,1)S(1)}) conditional(s32[]{:T(128)} %clamp.3, bf16[1,4096]{1,0:T(2,128)(2,1)S(1)} %pad_maximum_fusion.10, bf16[1,4096]{1,0:T(2,128)(2,1)S(1)} %pad_maximum_fusion.10, bf16[1,4096]{1,0:T(2,128)(2,1)S(1)} %pad_maximum_fusion.10, ...), branch_computations={%region_3.4_spmd, %region_4.5_spmd, %region_5.6_spmd, %region_6.7_... | conditional | flops 131072 | bytes 196776 | solution.py:191
  10.7 0.9 %collective-permute-start.35 = (bf16[1,4096]{1,0:T(2,128)(2,1)S(1)}, bf16[1,4096]{1,0:T(2,128)(2,1)S(1)}, u32[]{:S(2)}, u32[]{:S(2)}) collective-permute-start(bf16[1,4096]{1,0:T(2,128)(2,1)S(1)} %param.8), channel_id=1, source_target_pairs={{0,28},{4,24},{8,20},{12,16},{16,12},{20,8},{24,4},{28,0},{1,29},{... | collective-permute-start | bytes 24584 | tf_op jit(solution)/shard_map/cond/branch_8_fun/ppermute | solution.py:25
  11.5 1.7 %collective-permute-start.34 = (bf16[1,4096]{1,0:T(2,128)(2,1)S(1)}, bf16[1,4096]{1,0:T(2,128)(2,1)S(1)}, u32[]{:S(2)}, u32[]{:S(2)}) collective-permute-start(bf16[1,4096]{1,0:T(2,128)(2,1)S(1)} %param.8), channel_id=1, source_target_pairs={{0,24},{4,28},{8,16},{12,20},{16,8},{20,12},{24,0},{28,4},{1,25},{... | collective-permute-start | bytes 24584 | tf_op jit(solution)/shard_map/cond/branch_8_fun/ppermute | solution.py:25
  13.3 0.5 %collective-permute-start.33 = (bf16[1,4096]{1,0:T(2,128)(2,1)S(1)}, bf16[1,4096]{1,0:T(2,128)(2,1)S(1)}, u32[]{:S(2)}, u32[]{:S(2)}) collective-permute-start(bf16[1,4096]{1,0:T(2,128)(2,1)S(1)} %param.8), channel_id=1, source_target_pairs={{0,16},{4,20},{8,24},{12,28},{16,0},{20,4},{24,8},{28,12},{1,17},{... | collective-permute-start | bytes 24584 | tf_op jit(solution)/shard_map/cond/branch_8_fun/ppermute | solution.py:25
  13.8 1.0 %collective-permute-start.32 = (bf16[1,4096]{1,0:T(2,128)(2,1)S(1)}, bf16[1,4096]{1,0:T(2,128)(2,1)S(1)}, u32[]{:S(2)}, u32[]{:S(2)}) collective-permute-start(bf16[1,4096]{1,0:T(2,128)(2,1)S(1)} %param.8), channel_id=1, source_target_pairs={{0,4},{4,0},{8,12},{12,8},{16,20},{20,16},{24,28},{28,24},{1,5},{5... | collective-permute-start | bytes 24584 | tf_op jit(solution)/shard_map/cond/branch_8_fun/ppermute | solution.py:25
  14.7 0.1 collective-permute-done.35
  14.9 1.3 %collective-permute-done.34 = bf16[1,4096]{1,0:T(2,128)(2,1)S(1)} collective-permute-done((bf16[1,4096]{1,0:T(2,128)(2,1)S(1)}, bf16[1,4096]{1,0:T(2,128)(2,1)S(1)}, u32[]{:S(2)}, u32[]{:S(2)}) %collective-permute-start.34) | collective-permute-done | bytes 8224 | tf_op jit(solution)/shard_map/cond/branch_8_fun/ppermute | solution.py:25
  16.2 1.0 %collective-permute-done.33 = bf16[1,4096]{1,0:T(2,128)(2,1)S(1)} collective-permute-done((bf16[1,4096]{1,0:T(2,128)(2,1)S(1)}, bf16[1,4096]{1,0:T(2,128)(2,1)S(1)}, u32[]{:S(2)}, u32[]{:S(2)}) %collective-permute-start.33) | collective-permute-done | bytes 8224 | tf_op jit(solution)/shard_map/cond/branch_8_fun/ppermute | solution.py:25
  17.1 0.0 collective-permute-done.32
  17.1 0.1 pad_maximum_fusion.8
  17.2 3.3 %shard_map.28 = f32[1024,128]{1,0:T(8,128)} custom-call(s32[4]{0:T(128)S(1)} %convert_reduce_fusion.chosen_far, bf16[32,1024]{1,0:T(8,128)(2,1)S(1)} %copy-done, bf16[32,1024]{1,0:T(8,128)(2,1)S(1)} %collective-permute-done.40.refs_1_, bf16[32,1024]{1,0:T(8,128)(2,1)S(1)} %collective-permute-done.41.refs_2_, ...), custom_call_target="tpu_custom_call" | custom-call | tf_op jit(solution)/shard_map/pallas_call | solution.py:150
  (5 shorter events, 0.1 us)
Async XLA Ops:
  0.0 9.9 %copy-start = (bf16[32,1024]{1,0:T(8,128)(2,1)S(1)}, bf16[32,1024]{1,0:T(8,128)(2,1)}, u32[]{:S(2)}) copy-start(bf16[32,1024]{1,0:T(8,128)(2,1)} %refs_0_.1) | copy-start | bytes 196612
  0.0 9.9 %collective-permute-start.42 = (bf16[32,1024]{1,0:T(8,128)(2,1)}, bf16[32,1024]{1,0:T(8,128)(2,1)S(1)}, u32[]{:S(2)}, u32[]{:S(2)}) collective-permute-start(bf16[32,1024]{1,0:T(8,128)(2,1)} %refs_0_.1), channel_id=1, source_target_pairs={{0,2},{1,3},{2,0},{3,1},{4,6},{5,7},{6,4},{7,5},{8,10},{9,11},{10,... | collective-permute-start | bytes 196616 | tf_op jit(solution)/shard_map/ppermute | solution.py:25
  4.0 6.4 %collective-permute-start.41 = (bf16[32,1024]{1,0:T(8,128)(2,1)}, bf16[32,1024]{1,0:T(8,128)(2,1)S(1)}, u32[]{:S(2)}, u32[]{:S(2)}) collective-permute-start(bf16[32,1024]{1,0:T(8,128)(2,1)} %refs_0_.1), channel_id=1, source_target_pairs={{0,3},{1,2},{2,1},{3,0},{4,7},{5,6},{6,5},{7,4},{8,11},{9,10},{10,... | collective-permute-start | bytes 196616 | tf_op jit(solution)/shard_map/ppermute | solution.py:25
  5.4 5.2 %collective-permute-start.40 = (bf16[32,1024]{1,0:T(8,128)(2,1)}, bf16[32,1024]{1,0:T(8,128)(2,1)S(1)}, u32[]{:S(2)}, u32[]{:S(2)}) collective-permute-start(bf16[32,1024]{1,0:T(8,128)(2,1)} %refs_0_.1), channel_id=1, source_target_pairs={{0,1},{1,0},{2,3},{3,2},{4,5},{5,4},{6,7},{7,6},{8,9},{9,8},{10,11... | collective-permute-start | bytes 196616 | tf_op jit(solution)/shard_map/ppermute | solution.py:25
  10.7 4.2 %collective-permute-start.35 = (bf16[1,4096]{1,0:T(2,128)(2,1)S(1)}, bf16[1,4096]{1,0:T(2,128)(2,1)S(1)}, u32[]{:S(2)}, u32[]{:S(2)}) collective-permute-start(bf16[1,4096]{1,0:T(2,128)(2,1)S(1)} %param.8), channel_id=1, source_target_pairs={{0,28},{4,24},{8,20},{12,16},{16,12},{20,8},{24,4},{28,0},{1,29},{... | collective-permute-start | bytes 24584 | tf_op jit(solution)/shard_map/cond/branch_8_fun/ppermute | solution.py:25
  11.5 4.6 %collective-permute-start.34 = (bf16[1,4096]{1,0:T(2,128)(2,1)S(1)}, bf16[1,4096]{1,0:T(2,128)(2,1)S(1)}, u32[]{:S(2)}, u32[]{:S(2)}) collective-permute-start(bf16[1,4096]{1,0:T(2,128)(2,1)S(1)} %param.8), channel_id=1, source_target_pairs={{0,24},{4,28},{8,16},{12,20},{16,8},{20,12},{24,0},{28,4},{1,25},{... | collective-permute-start | bytes 24584 | tf_op jit(solution)/shard_map/cond/branch_8_fun/ppermute | solution.py:25
  13.3 3.9 %collective-permute-start.33 = (bf16[1,4096]{1,0:T(2,128)(2,1)S(1)}, bf16[1,4096]{1,0:T(2,128)(2,1)S(1)}, u32[]{:S(2)}, u32[]{:S(2)}) collective-permute-start(bf16[1,4096]{1,0:T(2,128)(2,1)S(1)} %param.8), channel_id=1, source_target_pairs={{0,16},{4,20},{8,24},{12,28},{16,0},{20,4},{24,8},{28,12},{1,17},{... | collective-permute-start | bytes 24584 | tf_op jit(solution)/shard_map/cond/branch_8_fun/ppermute | solution.py:25
  13.8 3.4 %collective-permute-start.32 = (bf16[1,4096]{1,0:T(2,128)(2,1)S(1)}, bf16[1,4096]{1,0:T(2,128)(2,1)S(1)}, u32[]{:S(2)}, u32[]{:S(2)}) collective-permute-start(bf16[1,4096]{1,0:T(2,128)(2,1)S(1)} %param.8), channel_id=1, source_target_pairs={{0,4},{4,0},{8,12},{12,8},{16,20},{20,16},{24,28},{28,24},{1,5},{5... | collective-permute-start | bytes 24584 | tf_op jit(solution)/shard_map/cond/branch_8_fun/ppermute | solution.py:25

commit v4 on v3

--- a/solution.py
+++ b/solution.py
@@ -15,7 +15,7 @@
 LAGS = 1024
 WIDTH = 64
 HALVES = 128 // WIDTH
-MOST_BRANCHES = 16
+MOST_BLOCKS = 8
 
 epsilon = 1e-06
 
@@ -32,8 +32,9 @@
 
 
 def stack_strain(keys, strain, stacked, wide):
-    channels, tile_len = strain[0].shape
+    channels, tile_len = wide[0].shape[0], strain[0].shape[1]
     length = len(keys) * tile_len
+    strain = [group.at[at : at + channels] for group in strain for at in range(0, group.shape[0], channels)]
     blocks = stacked.shape[0] // channels
     here = lax.axis_index("tm")
     row_count = blocks * WIDTH
@@ -83,13 +84,12 @@
         shifts[rows, length : length + 128] = jnp.where(mask, 0.0, last).astype(jnp.bfloat16)
 
 
-def correlate_kernel(keys, groups, chosen_far, *refs):
-    tiles = len(keys)
+def correlate_kernel(keys, row_keys, tiles, groups, chosen_far, *refs):
     strain, far, (out, *refs) = refs[:tiles], refs[tiles : tiles + groups], refs[tiles + groups :]
     mates, refs = refs[:groups], refs[groups:]
     chosen, mate, line, stacked, shifts, total, turned, ready, fetched, sent, *wide = refs
     row_count = out.shape[0]
-    channels, tile_len = strain[0].shape
+    channels, tile_len = out.shape[1] // ROUNDS, strain[0].shape[1]
     length = line.shape[1]
     here = lax.axis_index("tm")
 
@@ -103,7 +103,7 @@
     at = 0
     for group in mates:
         count = group.shape[0]
-        for k, key in enumerate(keys):
+        for k, key in enumerate(row_keys):
             mate[at : at + count, pl.ds(place(0, tile_len, here ^ key), tile_len)] = group[
                 :, k * tile_len : (k + 1) * tile_len
             ].astype(jnp.float32)
@@ -138,8 +138,9 @@
         copy.wait()
 
 
-def correlate(keys, chosen, strain, mates, row_count):
-    channels, tile_len = strain[0].shape
+def correlate(keys, row_keys, chosen, strain, mates, row_count):
+    rows, tile_len = strain[0].shape
+    channels = rows * len(strain) // len(keys)
     length = len(keys) * tile_len
     depth = length + 128
     stacked_rows = channels * row_count // WIDTH
@@ -148,7 +149,7 @@
     anywhere = pl.BlockSpec(memory_space=pl.ANY)
     widths = [length + 2 * MAX_LAG + 128] + [length + 2 * MAX_LAG] * (HALVES - 1)
     return pl.pallas_call(
-        functools.partial(correlate_kernel, keys, len(mates)),
+        functools.partial(correlate_kernel, keys, row_keys, len(strain), len(mates)),
         out_shape=jax.ShapeDtypeStruct((row_count, channels * ROUNDS), jnp.float32),
         in_specs=[anywhere]
         + [in_vmem] * len(strain)
@@ -172,20 +173,35 @@
     )(chosen, *strain, *mates)
 
 
+def pair_weights(count):
+    weights, sums = [], set()
+    value = 0
+    while len(weights) < count:
+        more = {value + weight for weight in weights}
+        if not more & sums and len(more) == len(weights):
+            weights.append(value)
+            sums |= more
+        value += 1
+    return weights
+
+
 def by_plan(plan, own):
     block_count = lax.axis_size("sta")
     middle = range(2, block_count - 1)
-    choices = list(itertools.combinations(middle, ROUNDS - 2))
-    ends = (plan == 1) | (plan == block_count - 1)
-    high = jnp.max(jnp.where(ends, 0, plan))
-    low = jnp.min(jnp.where(ends, block_count, plan))
-    first, span = low - 2, 2 * len(middle) - 1
-    index = ((first * (span - first)) >> 1) + high - low - 1
+    weights = dict(zip(middle, pair_weights(len(middle))))
+    choices = {weights[a] + weights[b]: (a, b) for a, b in itertools.combinations(middle, 2)}
+    least = min(choices)
+    index = sum(jnp.where(plan == key, weight, 0) for key, weight in weights.items())
+    index = jnp.sum(index) - least
 
     def branch(keys):
         return lambda own: jnp.concatenate([swap(own, "sta", key) for key in keys])
 
-    branches = [branch((1, *keys, block_count - 1)) for keys in choices]
+    last = block_count - 1
+    branches = [
+        branch((1, *choices.get(total, choices[least]), last))
+        for total in range(least, max(choices) + 1)
+    ]
     ranks = jnp.sum((plan[None, :] < plan[:, None]).astype(jnp.int32), axis=1)
     index, ranks = lax.optimization_barrier((index, ranks))
     return ranks, lax.switch(index, branches, own)
@@ -194,19 +210,30 @@
 def local(strain, plan):
     tile_count, block_count = lax.axis_size("tm"), lax.axis_size("sta")
     row_count = SOURCES * LAGS // tile_count
-    source = lax.axis_index("tm") * row_count // LAGS
-    order = sorted(range(tile_count), key=lambda k: (k > 1, k if k < 2 else -k))
-    tiles = [strain] + [swap(strain, "tm", k) for k in order[1:]]
-    row = source * (strain.shape[0] // SOURCES)
-    own = jnp.concatenate([lax.dynamic_slice_in_dim(tile, row, 1, 0) for tile in tiles], axis=1)
-    if math.comb(max(block_count - 3, 0), ROUNDS - 2) in range(1, MOST_BRANCHES + 1):
+    here = lax.axis_index("tm")
+
+    def source_row(tile, index):
+        row = index * row_count // LAGS * (strain.shape[0] // SOURCES)
+        return lax.dynamic_slice_in_dim(tile, row, 1, 0)
+
+    even, odd = list(range(0, tile_count, 2)), list(range(1, tile_count, 2))[::-1]
+    arrived = [swap(strain, "tm", key) for key in even[1:]]
+    rows = [swap(source_row(strain, here ^ key), "tm", key) for key in odd]
+    own = jnp.concatenate(
+        rows + [source_row(strain, here)] + [source_row(tile, here) for tile in arrived], axis=1
+    )
+    row_order = odd + even
+    tile_order = [key ^ 1 for key in even] + even
+    near = jnp.concatenate([strain, *arrived])
+    far = swap(near, "tm", 1)
+    if ROUNDS == 4 and 5 <= block_count <= MOST_BLOCKS:
         chosen, mates = by_plan(plan, own)
         mates = [mates]
     else:
         chosen = plan
         pair = jnp.concatenate([own, swap(own, "sta", 1)])
         mates = [pair] + [swap(pair, "sta", 2 * g) for g in range(1, block_count // 2)]
-    return correlate(order, chosen, tiles, mates, row_count)
+    return correlate(tile_order, row_order, chosen, [far, near], mates, row_count)
 
 
 def solution(mesh):

time: 20.4 us -> 19.6 us (0.961)
  starting transfers between devices: 9.68 us -> 11.6 us
  other arithmetic: 2.38 us -> 0.92 us
  between operations: 2.08 us -> 0.72 us
    ppermute x7 -> x8, starting transfers between devices: 9.68 us -> 11.6 us  [swap(): return lax.ppermute(block, axis, [(i, i ^ key) for i in range(count)])]
    reduce_max x1 -> x0, other arithmetic: 1.36 us -> none  [by_plan(): high = jnp.max(jnp.where(ends, 0, plan))]
    reduce_sum x1, other arithmetic: 0.91 us -> 0.18 us  [by_plan(): ranks = jnp.sum((plan[None, :] < plan[:, None]).astype(jnp.int32), axis=1)]
    reduce_sum x0 -> x1, other arithmetic: none -> 0.63 us  [by_plan(): index = jnp.sum(index) - least]
    ppermute x7 -> x8, waiting for transfers between devices: 2.98 us -> 2.94 us  [swap(): return lax.ppermute(block, axis, [(i, i ^ key) for i in range(count)])]
  transfers between devices with their start and end apart: 7 -> 8, of which waited for: 5 -> 4; matrix products, arithmetic and copies ran while one was open for 11% -> 5% of each run, Pallas kernels for 0% -> 0%
where the time goes in v4:
time: 19.6 us
  starting transfers between devices  11.6 us (59%)
  Pallas kernels  3.34 us (17%)
  waiting for transfers between devices  2.94 us (15%)
  other arithmetic  0.92 us (5%)
  between operations  0.72 us (4%)
    ppermute x8, starting transfers between devices, swap(): return lax.ppermute(block, axis, [(i, i ^ key) for i in range(count)])  11.6 us
    pallas_call x1, Pallas kernels, correlate(): pl.pallas_call(functools.partial(correlate_kernel, keys, row_keys, len(st...  3.34 us
    ppermute x8, waiting for transfers between devices, swap(): return lax.ppermute(block, axis, [(i, i ^ key) for i in range(count)])  2.94 us
    reduce_sum x1, other arithmetic, by_plan(): index = jnp.sum(index) - least  0.63 us
  transfers between devices with their start and end apart: 8, of which 4 were waited for; matrix products, arithmetic and copies ran while one was open for 5% of the time, Pallas kernels for 0%

profile of v4, /device:TPU:0, one launch (start us, length us, event | category | flops | bytes accessed | tf_op | source)
XLA Modules:
  0.0 19.6 jit_solution(17481590610538844535)
XLA Ops:
  0.0 4.0 %collective-permute-start.44 = (bf16[32,1024]{1,0:T(8,128)(2,1)}, bf16[32,1024]{1,0:T(8,128)(2,1)S(1)}, u32[]{:S(2)}, u32[]{:S(2)}) collective-permute-start(bf16[32,1024]{1,0:T(8,128)(2,1)} %param.13), channel_id=1, source_target_pairs={{0,2},{1,3},{2,0},{3,1},{4,6},{5,7},{6,4},{7,5},{8,10},{9,11},{10,... | collective-permute-start | bytes 196616 | tf_op jit(solution)/shard_map/ppermute | solution.py:25
  4.0 0.0 copy-done
  4.1 0.0 copy-start.1
  4.1 1.9 %collective-permute-start.46 = (bf16[1,1024]{1,0:T(2,128)(2,1)S(1)}, bf16[1,1024]{1,0:T(2,128)(2,1)S(1)}, u32[]{:S(2)}, u32[]{:S(2)}) collective-permute-start(bf16[1,1024]{1,0:T(2,128)(2,1)S(1)} %get-tuple-element.32), channel_id=1, source_target_pairs={{0,3},{1,2},{2,1},{3,0},{4,7},{5,6},{6,5},{7,4},{8,11},{9,10},{10,... | collective-permute-start | bytes 6152 | tf_op jit(solution)/shard_map/ppermute | solution.py:25
  6.0 0.0 collective-permute-start.47
  6.0 0.0 copy-done.1
  6.0 0.6 %fusion.3 = s32[]{:T(128)} fusion(s32[4]{0:T(128)S(1)} %copy-done.1), kind=kLoop, calls=%fused_computation.26 | loop fusion | flops 47 | bytes 20 | tf_op jit(solution)/shard_map/reduce_sum | solution.py:195
  6.6 0.2 convert_reduce_fusion.chosen_far
  7.5 0.5 %collective-permute-done.44 = bf16[32,1024]{1,0:T(8,128)(2,1)S(1)} collective-permute-done((bf16[32,1024]{1,0:T(8,128)(2,1)}, bf16[32,1024]{1,0:T(8,128)(2,1)S(1)}, u32[]{:S(2)}, u32[]{:S(2)}) %collective-permute-start.44) | collective-permute-done | bytes 65568 | tf_op jit(solution)/shard_map/ppermute | solution.py:25
  8.0 1.6 %collective-permute-start.45 = (bf16[64,1024]{1,0:T(8,128)(2,1)S(1)}, bf16[64,1024]{1,0:T(8,128)(2,1)S(1)}, u32[]{:S(2)}, u32[]{:S(2)}) collective-permute-start(bf16[64,1024]{1,0:T(8,128)(2,1)S(1)} %constant_dynamic-update-slice_fusion.refs_1_), channel_id=1, source_target_pairs={{0,1},{1,0},{2,3},{3,2},{4,5},{5,4},{6,7},{7,6},{8,9},{9,8},{10,11... | collective-permute-start | bytes 393224 | tf_op jit(solution)/shard_map/ppermute | solution.py:25
  9.6 0.0 collective-permute-done.46
  9.6 0.0 collective-permute-done.47
  9.7 6.6 %conditional.1 = (bf16[4,4096]{1,0:T(4,128)(2,1)S(1)}) conditional(s32[]{:T(128)} %clamp.3, bf16[1,4096]{1,0:T(2,128)(2,1)S(1)} %pad_maximum_fusion.11, bf16[1,4096]{1,0:T(2,128)(2,1)S(1)} %pad_maximum_fusion.11, bf16[1,4096]{1,0:T(2,128)(2,1)S(1)} %pad_maximum_fusion.11, ...), branch_computations={%region_2.3_spmd, %region_3.4_spmd, %region_4.5_spmd, %region_5.6_... | conditional | flops 131072 | bytes 196776 | solution.py:207
  9.7 1.1 %collective-permute-start.35 = (bf16[1,4096]{1,0:T(2,128)(2,1)S(1)}, bf16[1,4096]{1,0:T(2,128)(2,1)S(1)}, u32[]{:S(2)}, u32[]{:S(2)}) collective-permute-start(bf16[1,4096]{1,0:T(2,128)(2,1)S(1)} %param.8), channel_id=1, source_target_pairs={{0,28},{4,24},{8,20},{12,16},{16,12},{20,8},{24,4},{28,0},{1,29},{... | collective-permute-start | bytes 24584 | tf_op jit(solution)/shard_map/cond/branch_8_fun/ppermute | solution.py:25
  10.8 1.5 %collective-permute-start.34 = (bf16[1,4096]{1,0:T(2,128)(2,1)S(1)}, bf16[1,4096]{1,0:T(2,128)(2,1)S(1)}, u32[]{:S(2)}, u32[]{:S(2)}) collective-permute-start(bf16[1,4096]{1,0:T(2,128)(2,1)S(1)} %param.8), channel_id=1, source_target_pairs={{0,24},{4,28},{8,16},{12,20},{16,8},{20,12},{24,0},{28,4},{1,25},{... | collective-permute-start | bytes 24584 | tf_op jit(solution)/shard_map/cond/branch_8_fun/ppermute | solution.py:25
  12.3 0.5 %collective-permute-start.33 = (bf16[1,4096]{1,0:T(2,128)(2,1)S(1)}, bf16[1,4096]{1,0:T(2,128)(2,1)S(1)}, u32[]{:S(2)}, u32[]{:S(2)}) collective-permute-start(bf16[1,4096]{1,0:T(2,128)(2,1)S(1)} %param.8), channel_id=1, source_target_pairs={{0,16},{4,20},{8,24},{12,28},{16,0},{20,4},{24,8},{28,12},{1,17},{... | collective-permute-start | bytes 24584 | tf_op jit(solution)/shard_map/cond/branch_8_fun/ppermute | solution.py:25
  12.8 1.0 %collective-permute-start.32 = (bf16[1,4096]{1,0:T(2,128)(2,1)S(1)}, bf16[1,4096]{1,0:T(2,128)(2,1)S(1)}, u32[]{:S(2)}, u32[]{:S(2)}) collective-permute-start(bf16[1,4096]{1,0:T(2,128)(2,1)S(1)} %param.8), channel_id=1, source_target_pairs={{0,4},{4,0},{8,12},{12,8},{16,20},{20,16},{24,28},{28,24},{1,5},{5... | collective-permute-start | bytes 24584 | tf_op jit(solution)/shard_map/cond/branch_8_fun/ppermute | solution.py:25
  13.8 0.1 collective-permute-done.35
  13.9 1.6 %collective-permute-done.34 = bf16[1,4096]{1,0:T(2,128)(2,1)S(1)} collective-permute-done((bf16[1,4096]{1,0:T(2,128)(2,1)S(1)}, bf16[1,4096]{1,0:T(2,128)(2,1)S(1)}, u32[]{:S(2)}, u32[]{:S(2)}) %collective-permute-start.34) | collective-permute-done | bytes 8224 | tf_op jit(solution)/shard_map/cond/branch_8_fun/ppermute | solution.py:25
  15.5 0.7 %collective-permute-done.33 = bf16[1,4096]{1,0:T(2,128)(2,1)S(1)} collective-permute-done((bf16[1,4096]{1,0:T(2,128)(2,1)S(1)}, bf16[1,4096]{1,0:T(2,128)(2,1)S(1)}, u32[]{:S(2)}, u32[]{:S(2)}) %collective-permute-start.33) | collective-permute-done | bytes 8224 | tf_op jit(solution)/shard_map/cond/branch_8_fun/ppermute | solution.py:25
  16.2 0.0 collective-permute-done.32
  16.2 0.1 pad_maximum_fusion.8
  16.3 0.0 collective-permute-done.45.refs_0_
  16.3 3.3 %shard_map.28 = f32[1024,128]{1,0:T(8,128)} custom-call(s32[4]{0:T(128)S(1)} %convert_reduce_fusion.chosen_far, bf16[64,1024]{1,0:T(8,128)(2,1)S(1)} %collective-permute-done.45.refs_0_, bf16[64,1024]{1,0:T(8,128)(2,1)S(1)} %constant_dynamic-update-slice_fusion.refs_1_, bf16[4,4096]{1,0:T(4,128)(2,1)S(1)} %get-tuple-element.35.refs_2_), custom_call_target="tpu_custom_call" | custom-call | tf_op jit(solution)/shard_map/pallas_call | solution.py:151
  (6 shorter events, 0.1 us)
Async XLA Ops:
  0.0 4.0 %copy-start = (bf16[32,1024]{1,0:T(8,128)(2,1)S(1)}, bf16[32,1024]{1,0:T(8,128)(2,1)}, u32[]{:S(2)}) copy-start(bf16[32,1024]{1,0:T(8,128)(2,1)} %param.13) | copy-start | bytes 196612
  0.0 8.0 %collective-permute-start.44 = (bf16[32,1024]{1,0:T(8,128)(2,1)}, bf16[32,1024]{1,0:T(8,128)(2,1)S(1)}, u32[]{:S(2)}, u32[]{:S(2)}) collective-permute-start(bf16[32,1024]{1,0:T(8,128)(2,1)} %param.13), channel_id=1, source_target_pairs={{0,2},{1,3},{2,0},{3,1},{4,6},{5,7},{6,4},{7,5},{8,10},{9,11},{10,... | collective-permute-start | bytes 196616 | tf_op jit(solution)/shard_map/ppermute | solution.py:25
  4.1 1.9 %copy-start.1 = (s32[4]{0:T(128)S(1)}, s32[4]{0:T(128)}, u32[]{:S(2)}) copy-start(s32[4]{0:T(128)} %param.14) | copy-start | bytes 52
  4.1 5.5 %collective-permute-start.46 = (bf16[1,1024]{1,0:T(2,128)(2,1)S(1)}, bf16[1,1024]{1,0:T(2,128)(2,1)S(1)}, u32[]{:S(2)}, u32[]{:S(2)}) collective-permute-start(bf16[1,1024]{1,0:T(2,128)(2,1)S(1)} %get-tuple-element.32), channel_id=1, source_target_pairs={{0,3},{1,2},{2,1},{3,0},{4,7},{5,6},{6,5},{7,4},{8,11},{9,10},{10,... | collective-permute-start | bytes 6152 | tf_op jit(solution)/shard_map/ppermute | solution.py:25
  6.0 3.6 %collective-permute-start.47 = (bf16[1,1024]{1,0:T(2,128)(2,1)S(1)}, bf16[1,1024]{1,0:T(2,128)(2,1)S(1)}, u32[]{:S(2)}, u32[]{:S(2)}) collective-permute-start(bf16[1,1024]{1,0:T(2,128)(2,1)S(1)} %get-tuple-element.34), channel_id=1, source_target_pairs={{0,1},{1,0},{2,3},{3,2},{4,5},{5,4},{6,7},{7,6},{8,9},{9,8},{10,11... | collective-permute-start | bytes 6152 | tf_op jit(solution)/shard_map/ppermute | solution.py:25
  8.0 8.3 %collective-permute-start.45 = (bf16[64,1024]{1,0:T(8,128)(2,1)S(1)}, bf16[64,1024]{1,0:T(8,128)(2,1)S(1)}, u32[]{:S(2)}, u32[]{:S(2)}) collective-permute-start(bf16[64,1024]{1,0:T(8,128)(2,1)S(1)} %constant_dynamic-update-slice_fusion.refs_1_), channel_id=1, source_target_pairs={{0,1},{1,0},{2,3},{3,2},{4,5},{5,4},{6,7},{7,6},{8,9},{9,8},{10,11... | collective-permute-start | bytes 393224 | tf_op jit(solution)/shard_map/ppermute | solution.py:25
  9.7 4.2 %collective-permute-start.35 = (bf16[1,4096]{1,0:T(2,128)(2,1)S(1)}, bf16[1,4096]{1,0:T(2,128)(2,1)S(1)}, u32[]{:S(2)}, u32[]{:S(2)}) collective-permute-start(bf16[1,4096]{1,0:T(2,128)(2,1)S(1)} %param.8), channel_id=1, source_target_pairs={{0,28},{4,24},{8,20},{12,16},{16,12},{20,8},{24,4},{28,0},{1,29},{... | collective-permute-start | bytes 24584 | tf_op jit(solution)/shard_map/cond/branch_8_fun/ppermute | solution.py:25
  10.8 4.7 %collective-permute-start.34 = (bf16[1,4096]{1,0:T(2,128)(2,1)S(1)}, bf16[1,4096]{1,0:T(2,128)(2,1)S(1)}, u32[]{:S(2)}, u32[]{:S(2)}) collective-permute-start(bf16[1,4096]{1,0:T(2,128)(2,1)S(1)} %param.8), channel_id=1, source_target_pairs={{0,24},{4,28},{8,16},{12,20},{16,8},{20,12},{24,0},{28,4},{1,25},{... | collective-permute-start | bytes 24584 | tf_op jit(solution)/shard_map/cond/branch_8_fun/ppermute | solution.py:25
  12.3 3.9 %collective-permute-start.33 = (bf16[1,4096]{1,0:T(2,128)(2,1)S(1)}, bf16[1,4096]{1,0:T(2,128)(2,1)S(1)}, u32[]{:S(2)}, u32[]{:S(2)}) collective-permute-start(bf16[1,4096]{1,0:T(2,128)(2,1)S(1)} %param.8), channel_id=1, source_target_pairs={{0,16},{4,20},{8,24},{12,28},{16,0},{20,4},{24,8},{28,12},{1,17},{... | collective-permute-start | bytes 24584 | tf_op jit(solution)/shard_map/cond/branch_8_fun/ppermute | solution.py:25
  12.8 3.4 %collective-permute-start.32 = (bf16[1,4096]{1,0:T(2,128)(2,1)S(1)}, bf16[1,4096]{1,0:T(2,128)(2,1)S(1)}, u32[]{:S(2)}, u32[]{:S(2)}) collective-permute-start(bf16[1,4096]{1,0:T(2,128)(2,1)S(1)} %param.8), channel_id=1, source_target_pairs={{0,4},{4,0},{8,12},{12,8},{16,20},{20,16},{24,28},{28,24},{1,5},{5... | collective-permute-start | bytes 24584 | tf_op jit(solution)/shard_map/cond/branch_8_fun/ppermute | solution.py:25
